TPU v7x, 128 devices: a whole 4x4x4 slice. The times are simulated.
128 devices in a mesh: head: 8 (over z, core), seq: 16 (over x, y).
Axes of the slice: x: 4, y: 4, z: 4, core: 2. Of those that a mesh axis runs over, the one named last changes fastest.
Arguments:
- queries: bfloat16 [16384, 16, 128], P('seq', 'head'), may hold values from -14 to 14
- keys: bfloat16 [16384, 16, 128], P('seq', 'head'), may hold values from -14 to 14
- values: bfloat16 [16384, 16, 128], P('seq', 'head'), may hold values from -6 to 6
- out_grad: bfloat16 [16384, 16, 128], P('seq', 'head'), may hold values from -6 to 6
- cluster_ids: int32 [16, 16384, 1], P('head', 'seq'), may hold values from 0 to 191; in each aligned block of 1024 rows (0 to 1023, 1024 to 2047, ..., all dimensions but the last counted through in order) at most 8 rows name the same one
- query_weight: bfloat16 [2048, 16, 128], P(None, 'head'), may hold values from -0.125 to 0.125
- key_weight: bfloat16 [2048, 16, 128], P(None, 'head'), may hold values from -0.125 to 0.125
- value_weight: bfloat16 [2048, 16, 128], P(None, 'head'), may hold values from -0.125 to 0.125
Outputs:
- query_gradient: bfloat16 [16384, 16, 128], P('seq', 'head')
- key_gradient: bfloat16 [16384, 16, 128], P('seq', 'head')
- value_gradient: bfloat16 [16384, 16, 128], P('seq', 'head')
- input_grad: bfloat16 [2048, 16384], P('head', 'seq')
- key_sums: float32 [16, 192, 128], P('head', 'seq')
Inputs may be any that keep to these rules, and one draw needn't show every extreme that they name: `cluster_ids`: in each head, no cluster holds more than 8 of the tokens of one index of seq.
All inputs are finite; a program needn't handle non-finite values.
Results may differ from a plain program's by a relative error of at most 0.028.
The roundings to bfloat16 on the way count: a program that leaves them out, or rounds other values in their place, can miss the bound.
Values may be sent and summed in bfloat16 or wider, within the bound.
No kernel may reach another device: no remote copies, remote signals or barrier semaphores. Data moves between devices by JAX's collectives and lax.ppermute only.
A program may use at most 64 MiB of HBM per device.

v0:
```python
import math

import jax
import jax.numpy as jnp
from jax import lax
from jax.sharding import PartitionSpec as P

CLUSTERS = 192
SLOTS = 8


def shards(queries, keys, values, out_grad, cluster_ids, query_weight, key_weight, value_weight):
    seq_count = lax.axis_size("seq")
    tok, heads_dev, width = queries.shape
    cl_dev = CLUSTERS // seq_count
    capacity = SLOTS * seq_count
    slot_total = cl_dev * capacity
    scale = 1.0 / math.sqrt(width)
    ids = cluster_ids[:, :, 0]
    onehot = ids[:, :, None] == jnp.arange(CLUSTERS, dtype=jnp.int32)[None, None, :]
    onehot_b = onehot.astype(jnp.bfloat16)
    counts = jnp.sum(onehot.astype(jnp.int32), axis=1)
    tok_pos = jnp.arange(tok, dtype=jnp.int32)
    earlier = (tok_pos[None, :] < tok_pos[:, None]).astype(jnp.bfloat16)
    before = jnp.einsum("tu,huc->htc", earlier, onehot_b, preferred_element_type=jnp.float32)
    rank = jnp.sum(jnp.where(onehot, before, jnp.float32(0.0)), axis=-1).astype(jnp.int32)
    flat = ids % cl_dev * capacity + ids // cl_dev * SLOTS + rank
    placing = (flat[:, None, :] == jnp.arange(slot_total, dtype=jnp.int32)[None, :, None]).astype(
        jnp.bfloat16
    )

    def pack(tensor):
        spread = jnp.einsum(
            "hst,thd->hsd", placing, tensor, preferred_element_type=jnp.float32
        ).astype(jnp.bfloat16)
        return spread.reshape(heads_dev, cl_dev, capacity, width)

    def unpack(buffer):
        rows = buffer.reshape(buffer.shape[0], slot_total, width)
        return jnp.einsum("hst,hsd->thd", placing, rows, preferred_element_type=jnp.float32).astype(
            jnp.bfloat16
        )

    sent_counts = jnp.transpose(counts.reshape(heads_dev, seq_count, cl_dev), (0, 2, 1)).astype(
        jnp.bfloat16
    )
    position = jnp.arange(capacity, dtype=jnp.int32)
    causal = position[None, :] <= position[:, None]
    diagonal = position[None, :] == position[:, None]
    q_buf = lax.all_to_all(pack(queries), "seq", split_axis=2, concat_axis=2, tiled=True)
    k_buf = lax.all_to_all(pack(keys), "seq", split_axis=2, concat_axis=2, tiled=True)
    v_buf = lax.all_to_all(pack(values), "seq", split_axis=2, concat_axis=2, tiled=True)
    g_buf = lax.all_to_all(pack(out_grad), "seq", split_axis=2, concat_axis=2, tiled=True)
    got_counts = lax.all_to_all(sent_counts, "seq", split_axis=2, concat_axis=2, tiled=True)
    items = q_buf.shape[0]
    live = (
        jnp.arange(SLOTS, dtype=jnp.int32)[None, None, None, :]
        < got_counts.astype(jnp.int32)[..., None]
    )
    live = live.reshape(items, cl_dev, capacity)
    allowed = causal[None, None] & live[:, :, None, :] | diagonal[None, None]
    scores = jnp.einsum("hcqd,hckd->hcqk", q_buf, k_buf, preferred_element_type=jnp.float32) * scale
    scores = jnp.where(allowed, scores, jnp.float32(-1e30))
    top = jnp.max(scores, axis=-1, keepdims=True)
    expo = jnp.where(allowed, jnp.exp(scores - top), jnp.float32(0.0))
    probs = expo / jnp.sum(expo, axis=-1, keepdims=True)
    probs_b = probs.astype(jnp.bfloat16)
    attended = jnp.einsum("hcqk,hckd->hcqd", probs_b, v_buf, preferred_element_type=jnp.float32)
    delta = jnp.sum(g_buf.astype(jnp.float32) * attended, axis=-1)
    dprob = jnp.einsum("hcqd,hckd->hcqk", g_buf, v_buf, preferred_element_type=jnp.float32)
    dscore = (probs * (dprob - delta[..., None]) * scale).astype(jnp.bfloat16)
    grad_q = jnp.einsum(
        "hcqk,hckd->hcqd", dscore, k_buf, preferred_element_type=jnp.float32
    ).astype(jnp.bfloat16)
    grad_k = jnp.einsum(
        "hcqk,hcqd->hckd", dscore, q_buf, preferred_element_type=jnp.float32
    ).astype(jnp.bfloat16)
    grad_v = jnp.einsum(
        "hcqk,hcqd->hckd", probs_b, g_buf, preferred_element_type=jnp.float32
    ).astype(jnp.bfloat16)
    query_gradient = unpack(lax.all_to_all(grad_q, "seq", split_axis=2, concat_axis=2, tiled=True))
    key_gradient = unpack(lax.all_to_all(grad_k, "seq", split_axis=2, concat_axis=2, tiled=True))
    value_gradient = unpack(lax.all_to_all(grad_v, "seq", split_axis=2, concat_axis=2, tiled=True))
    local_sums = jnp.einsum("htc,thd->hcd", onehot_b, keys, preferred_element_type=jnp.float32)
    key_total = lax.psum_scatter(
        local_sums.astype(jnp.bfloat16), "seq", scatter_dimension=1, tiled=True
    ).astype(jnp.float32)
    key_sums = key_total / math.sqrt(capacity)
    grand_total = jnp.einsum(
        "eny,lny->el", query_weight, query_gradient, preferred_element_type=jnp.float32
    )
    grand_total = grand_total + jnp.einsum(
        "eny,lny->el", key_weight, key_gradient, preferred_element_type=jnp.float32
    )
    input_grad = lax.psum_scatter(
        (
            grand_total
            + jnp.einsum(
                "eny,lny->el", value_weight, value_gradient, preferred_element_type=jnp.float32
            )
        ).astype(jnp.bfloat16),
        "head",
        scatter_dimension=0,
        tiled=True,
    )
    return (query_gradient, key_gradient, value_gradient, input_grad, key_sums)


def solution(mesh):
    placed = (
        P("seq", "head", None),
        P("seq", "head", None),
        P("seq", "head", None),
        P("seq", "head", None),
        P("head", "seq", None),
        P(None, "head", None),
        P(None, "head", None),
        P(None, "head", None),
    )
    return jax.shard_map(
        shards,
        mesh=mesh,
        in_specs=placed,
        out_specs=(
            P("seq", "head", None),
            P("seq", "head", None),
            P("seq", "head", None),
            P("head", "seq"),
            P("head", "seq", None),
        ),
        check_vma=False,
    )
```

profile of v0, /device:TPU:0, one launch (start us, length us, event | category | flops | bytes accessed | tf_op | source)
XLA Modules:
  0.0 237.9 jit_solution(1905787048986860312)
XLA Ops:
  9.8 7.1 %all-to-all-start = ((bf16[2,12,16]{1,0,2:T(2,128)(2,1)}), bf16[2,12,16]{1,0,2:T(2,128)(2,1)S(1)}, u32[]{:S(2)}, u32[]{:S(2)}) async-start(bf16[2,12,16]{1,0,2:T(2,128)(2,1)} %copy.192), calls=%async_computation | async-start | bytes 16384 | tf_op jit(solution)/shard_map/all_to_all | solution.py:54
  18.0 2.3 fusion.21
  20.3 1.7 copy.196
  22.1 2.3 all-to-all-done
  24.4 4.9 %all-to-all-start.1 = ((bf16[2,12,128,128]{3,0,1,2:T(2,128)(2,1)}), bf16[2,12,128,128]{3,0,1,2:T(2,128)(2,1)S(1)}, u32[]{:S(2)}, u32[]{:S(2)}) async-start(bf16[2,12,128,128]{3,0,1,2:T(2,128)(2,1)} %copy.196), calls=%async_computation.1 | async-start | bytes 1572864 | tf_op jit(solution)/shard_map/all_to_all | solution.py:50
  29.3 2.3 fusion.22
  33.3 9.7 %all-to-all-done.1 = bf16[2,12,128,128]{3,0,1,2:T(2,128)(2,1)S(1)} async-done(((bf16[2,12,128,128]{3,0,1,2:T(2,128)(2,1)}), bf16[2,12,128,128]{3,0,1,2:T(2,128)(2,1)S(1)}, u32[]{:S(2)}, u32[]{:S(2)}) %all-to-all-start.1) | async-done | bytes 786464 | tf_op jit(solution)/shard_map/all_to_all | solution.py:50
  43.0 4.5 %all-to-all-start.2 = ((bf16[2,12,128,128]{3,0,1,2:T(2,128)(2,1)}), bf16[2,12,128,128]{3,0,1,2:T(2,128)(2,1)}, u32[]{:S(2)}, u32[]{:S(2)}) async-start(bf16[2,12,128,128]{3,0,1,2:T(2,128)(2,1)} %copy.198), calls=%async_computation.2 | async-start | bytes 1572864 | tf_op jit(solution)/shard_map/all_to_all | solution.py:51
  47.5 2.3 fusion.23
  51.5 8.6 %all-to-all-done.2 = bf16[2,12,128,128]{3,0,1,2:T(2,128)(2,1)} async-done(((bf16[2,12,128,128]{3,0,1,2:T(2,128)(2,1)}), bf16[2,12,128,128]{3,0,1,2:T(2,128)(2,1)}, u32[]{:S(2)}, u32[]{:S(2)}) %all-to-all-start.2) | async-done | bytes 786464 | tf_op jit(solution)/shard_map/all_to_all | solution.py:51
  60.1 3.6 %all-to-all-start.3 = ((bf16[2,12,128,128]{3,0,1,2:T(2,128)(2,1)}), bf16[2,12,128,128]{3,0,1,2:T(2,128)(2,1)S(1)}, u32[]{:S(2)}, u32[]{:S(2)}) async-start(bf16[2,12,128,128]{3,0,1,2:T(2,128)(2,1)} %copy.202), calls=%async_computation.3 | async-start | bytes 1572864 | tf_op jit(solution)/shard_map/all_to_all | solution.py:53
  63.8 2.3 fusion.24
  68.2 7.1 %all-to-all-done.3 = bf16[2,12,128,128]{3,0,1,2:T(2,128)(2,1)S(1)} async-done(((bf16[2,12,128,128]{3,0,1,2:T(2,128)(2,1)}), bf16[2,12,128,128]{3,0,1,2:T(2,128)(2,1)S(1)}, u32[]{:S(2)}, u32[]{:S(2)}) %all-to-all-start.3) | async-done | bytes 786464 | tf_op jit(solution)/shard_map/all_to_all | solution.py:53
  75.3 3.6 %all-to-all-start.4 = ((bf16[2,12,128,128]{3,0,1,2:T(2,128)(2,1)}), bf16[2,12,128,128]{3,0,1,2:T(2,128)(2,1)S(1)}, u32[]{:S(2)}, u32[]{:S(2)}) async-start(bf16[2,12,128,128]{3,0,1,2:T(2,128)(2,1)} %copy.204), calls=%async_computation.4 | async-start | bytes 1572864 | tf_op jit(solution)/shard_map/all_to_all | solution.py:52
  79.7 3.6 %fusion.61 = (f32[2,12,128]{2,1,0:T(8,128)S(1)}, f32[2,12,128,128]{2,3,1,0:T(8,128)}) fusion(pred[128,128]{0,1:T(8,128)(4,1)S(1)} %get-tuple-element.37, pred[2,12,128]{2,1,0:T(8,128)(4,1)S(1)} %copy.194, pred[128,128]{0,1:T(8,128)(4,1)S(1)} %get-tuple-element.38, bf16[2,12,128,128]{3,0,1,2:T(2,128)(2,1)} %all-to-all-done.2, ...), kind=kOutput, calls=%fused_computation.80 | convolution fusion | flops 104202368 | bytes 3193856 | tf_op jit(solution)/shard_map/sub | solution.py:65
  84.9 5.5 %all-to-all-done.4 = bf16[2,12,128,128]{3,0,1,2:T(2,128)(2,1)S(1)} async-done(((bf16[2,12,128,128]{3,0,1,2:T(2,128)(2,1)}), bf16[2,12,128,128]{3,0,1,2:T(2,128)(2,1)S(1)}, u32[]{:S(2)}, u32[]{:S(2)}) %all-to-all-start.4) | async-done | bytes 786464 | tf_op jit(solution)/shard_map/all_to_all | solution.py:52
  90.4 1.9 copy.209
  92.2 2.7 %fusion = f32[2,12,128,128]{2,3,1,0:T(8,128)} fusion(bf16[2,12,128,128]{2,3,1,0:T(8,128)(2,1)S(1)} %copy.207, bf16[2,12,128,128]{2,3,1,0:T(8,128)(2,1)} %copy.209, bf16[2,12,128,128]{2,3,1,0:T(8,128)(2,1)S(1)} %fusion.50), kind=kOutput, calls=%fused_computation | convolution fusion | flops 101452928 | bytes 3932160 | tf_op jit(solution)/shard_map/sub | solution.py:71
  95.0 2.5 %multiply_convert_fusion = bf16[2,12,128,128]{2,3,1,0:T(8,128)(2,1)S(1)} fusion(f32[2,12,128,128]{2,3,1,0:T(8,128)} %fusion, bf16[2,12,128,128]{2,3,1,0:T(8,128)(2,1)S(1)} %copy.207, bf16[2,12,128,128]{2,3,1,0:T(8,128)(2,1)S(1)} %copy-done.4, f32[2,12,128,128]{2,3,1,0:T(8,128)} %get-tuple-element.36, f32[2,12,128]{2,1,0:T(8,128)S(1)} %get-tuple-element.35), kind=kOutput, calls=%fused_computation.31 | convolution fusion | flops 102629376 | bytes 5517312 | tf_op jit(solution)/shard_map/hcqd,hckd->hcqk/dot_general | solution.py:70
  100.1 3.6 %all-to-all-start.6 = ((bf16[2,12,128,128]{3,0,1,2:T(2,128)(2,1)}), bf16[2,12,128,128]{3,0,1,2:T(2,128)(2,1)S(1)}, u32[]{:S(2)}, u32[]{:S(2)}) async-start(bf16[2,12,128,128]{3,0,1,2:T(2,128)(2,1)} %copy.217), calls=%async_computation.6 | async-start | bytes 1572864 | tf_op jit(solution)/shard_map/all_to_all | solution.py:82
  103.7 1.8 convolution_convert_fusion.2
  107.3 7.9 %all-to-all-done.6 = bf16[2,12,128,128]{3,0,1,2:T(2,128)(2,1)S(1)} async-done(((bf16[2,12,128,128]{3,0,1,2:T(2,128)(2,1)}), bf16[2,12,128,128]{3,0,1,2:T(2,128)(2,1)S(1)}, u32[]{:S(2)}, u32[]{:S(2)}) %all-to-all-start.6) | async-done | bytes 786464 | tf_op jit(solution)/shard_map/all_to_all | solution.py:82
  115.2 4.3 %all-to-all-start.5 = ((bf16[2,12,128,128]{3,0,1,2:T(2,128)(2,1)}), bf16[2,12,128,128]{3,0,1,2:T(2,128)(2,1)}, u32[]{:S(2)}, u32[]{:S(2)}) async-start(bf16[2,12,128,128]{3,0,1,2:T(2,128)(2,1)} %copy.213), calls=%async_computation.5 | async-start | bytes 1572864 | tf_op jit(solution)/shard_map/all_to_all | solution.py:81
  121.9 9.1 %all-to-all-done.5 = bf16[2,12,128,128]{3,0,1,2:T(2,128)(2,1)} async-done(((bf16[2,12,128,128]{3,0,1,2:T(2,128)(2,1)}), bf16[2,12,128,128]{3,0,1,2:T(2,128)(2,1)}, u32[]{:S(2)}, u32[]{:S(2)}) %all-to-all-start.5) | async-done | bytes 786464 | tf_op jit(solution)/shard_map/all_to_all | solution.py:81
  131.0 3.6 %all-to-all-start.7 = ((bf16[2,12,128,128]{3,0,1,2:T(2,128)(2,1)}), bf16[2,12,128,128]{3,0,1,2:T(2,128)(2,1)S(1)}, u32[]{:S(2)}, u32[]{:S(2)}) async-start(bf16[2,12,128,128]{3,0,1,2:T(2,128)(2,1)} %copy.221), calls=%async_computation.7 | async-start | bytes 1572864 | tf_op jit(solution)/shard_map/all_to_all | solution.py:83
  137.6 2.5 %fusion.34 = bf16[1024,2,128]{0,2,1:T(8,128)(2,1)S(1)} fusion(bf16[2,1536,128]{2,1,0:T(8,128)(2,1)S(1)} %bitcast.65, s32[2,1024]{1,0:T(2,128)S(1)} %fusion.58), kind=kOutput, calls=%fused_computation.48 | convolution fusion | flops 808714240 | bytes 1318912 | tf_op jit(solution)/shard_map/hst,hsd->thd/dot_general | solution.py:40
  140.1 2.5 %fusion.35 = bf16[1024,2,128]{0,2,1:T(8,128)(2,1)S(1)} fusion(bf16[2,1536,128]{2,1,0:T(8,128)(2,1)S(1)} %bitcast.66, s32[2,1024]{1,0:T(2,128)S(1)} %fusion.58), kind=kOutput, calls=%fused_computation.49 | convolution fusion | flops 808714240 | bytes 1318912 | tf_op jit(solution)/shard_map/hst,hsd->thd/dot_general | solution.py:40
  142.6 3.5 %all-to-all-done.7 = bf16[2,12,128,128]{3,0,1,2:T(2,128)(2,1)S(1)} async-done(((bf16[2,12,128,128]{3,0,1,2:T(2,128)(2,1)}), bf16[2,12,128,128]{3,0,1,2:T(2,128)(2,1)S(1)}, u32[]{:S(2)}, u32[]{:S(2)}) %all-to-all-start.7) | async-done | bytes 786464 | tf_op jit(solution)/shard_map/all_to_all | solution.py:83
  146.3 2.5 %fusion.33 = bf16[1024,2,128]{0,2,1:T(8,128)(2,1)S(1)} fusion(bf16[2,1536,128]{2,1,0:T(8,128)(2,1)S(1)} %bitcast.67, s32[2,1024]{1,0:T(2,128)S(1)} %fusion.58), kind=kOutput, calls=%fused_computation.47 | convolution fusion | flops 808714240 | bytes 1318912 | tf_op jit(solution)/shard_map/hst,hsd->thd/dot_general | solution.py:40
  151.4 3.4 %fusion.20 = bf16[2048,1024]{0,1:T(8,128)(2,1)} fusion(bf16[1024,2,128]{0,2,1:T(8,128)(2,1)S(1)} %fusion.33, f32[1024,2048,1]{1,0,2:T(8,128)S(1)} %fusion.40, f32[1024,2048,1]{1,0,2:T(8,128)S(1)} %fusion.42, bf16[2048,2,128]{2,1,0:T(2,128)(2,1)S(1)} %copy-done.6), kind=kOutput, calls=%fused_computation.23 | convolution fusion | flops 1080033280 | bytes 22544384 | tf_op jit(solution)/shard_map/eny,lny->el/dot_general | solution.py:98
  156.7 67.1 %all-reduce.3.cloned.1.call-done = bf16[2,192,128]{2,0,1:T(2,128)(2,1)} async-done(((bf16[2,192,128]{2,0,1:T(2,128)(2,1)}), bf16[2,192,128]{2,0,1:T(2,128)(2,1)}) %all-reduce.3.cloned.1.call-update) | async-done | bytes 98320
  228.4 2.0 copy.235
  (71 shorter events, 29.1 us)
Async XLA Ops:
  8.0 140.7 %copy-start = (bf16[2048,2,128]{2,1,0:T(2,128)(2,1)S(1)}, bf16[2048,2,128]{2,1,0:T(2,128)(2,1)}, u32[]{:S(2)}) copy-start(bf16[2048,2,128]{2,1,0:T(2,128)(2,1)} %param.14) | copy-start | bytes 3145732
  9.8 14.6 %all-to-all-start = ((bf16[2,12,16]{1,0,2:T(2,128)(2,1)}), bf16[2,12,16]{1,0,2:T(2,128)(2,1)S(1)}, u32[]{:S(2)}, u32[]{:S(2)}) async-start(bf16[2,12,16]{1,0,2:T(2,128)(2,1)} %copy.192), calls=%async_computation | async-start | bytes 16384 | tf_op jit(solution)/shard_map/all_to_all | solution.py:54
  16.9 1.1 copy-start.7
  16.9 1.1 copy-start.8
  20.3 9.0 %copy-start.11 = (bf16[1024,2,128]{2,1,0:T(2,128)(2,1)S(1)}, bf16[1024,2,128]{2,1,0:T(2,128)(2,1)}, u32[]{:S(2)}) copy-start(bf16[1024,2,128]{2,1,0:T(2,128)(2,1)} %param.9) | copy-start | bytes 1572868
  24.4 18.6 %all-to-all-start.1 = ((bf16[2,12,128,128]{3,0,1,2:T(2,128)(2,1)}), bf16[2,12,128,128]{3,0,1,2:T(2,128)(2,1)S(1)}, u32[]{:S(2)}, u32[]{:S(2)}) async-start(bf16[2,12,128,128]{3,0,1,2:T(2,128)(2,1)} %copy.196), calls=%async_computation.1 | async-start | bytes 1572864 | tf_op jit(solution)/shard_map/all_to_all | solution.py:50
  31.6 15.9 %copy-start.9 = (bf16[1024,2,128]{2,1,0:T(2,128)(2,1)S(1)}, bf16[1024,2,128]{2,1,0:T(2,128)(2,1)}, u32[]{:S(2)}) copy-start(bf16[1024,2,128]{2,1,0:T(2,128)(2,1)} %param.11) | copy-start | bytes 1572868
  43.0 8.5 %copy-start.1 = (bf16[2,12,128,128]{3,0,1,2:T(2,128)(2,1)}, bf16[2,12,128,128]{3,0,1,2:T(2,128)(2,1)S(1)}, u32[]{:S(2)}) copy-start(bf16[2,12,128,128]{3,0,1,2:T(2,128)(2,1)S(1)} %all-to-all-done.1) | copy-start | bytes 2359300
  43.0 17.1 %all-to-all-start.2 = ((bf16[2,12,128,128]{3,0,1,2:T(2,128)(2,1)}), bf16[2,12,128,128]{3,0,1,2:T(2,128)(2,1)}, u32[]{:S(2)}, u32[]{:S(2)}) async-start(bf16[2,12,128,128]{3,0,1,2:T(2,128)(2,1)} %copy.198), calls=%async_computation.2 | async-start | bytes 1572864 | tf_op jit(solution)/shard_map/all_to_all | solution.py:51
  49.8 14.0 %copy-start.10 = (bf16[1024,2,128]{2,1,0:T(2,128)(2,1)S(1)}, bf16[1024,2,128]{2,1,0:T(2,128)(2,1)}, u32[]{:S(2)}) copy-start(bf16[1024,2,128]{2,1,0:T(2,128)(2,1)} %param.10) | copy-start | bytes 1572868
  60.1 15.2 %all-to-all-start.3 = ((bf16[2,12,128,128]{3,0,1,2:T(2,128)(2,1)}), bf16[2,12,128,128]{3,0,1,2:T(2,128)(2,1)S(1)}, u32[]{:S(2)}, u32[]{:S(2)}) async-start(bf16[2,12,128,128]{3,0,1,2:T(2,128)(2,1)} %copy.202), calls=%async_computation.3 | async-start | bytes 1572864 | tf_op jit(solution)/shard_map/all_to_all | solution.py:53
  75.3 15.1 %all-to-all-start.4 = ((bf16[2,12,128,128]{3,0,1,2:T(2,128)(2,1)}), bf16[2,12,128,128]{3,0,1,2:T(2,128)(2,1)S(1)}, u32[]{:S(2)}, u32[]{:S(2)}) async-start(bf16[2,12,128,128]{3,0,1,2:T(2,128)(2,1)} %copy.204), calls=%async_computation.4 | async-start | bytes 1572864 | tf_op jit(solution)/shard_map/all_to_all | solution.py:52
  92.2 2.7 %copy-start.4 = (bf16[2,12,128,128]{2,3,1,0:T(8,128)(2,1)S(1)}, bf16[2,12,128,128]{2,3,1,0:T(8,128)(2,1)}, u32[]{:S(2)}) copy-start(bf16[2,12,128,128]{2,3,1,0:T(8,128)(2,1)} %copy.209) | copy-start | bytes 2359300
  95.0 2.5 %copy-start.2 = (bf16[2,12,128,128]{3,0,1,2:T(2,128)(2,1)S(1)}, bf16[2,12,128,128]{3,0,1,2:T(2,128)(2,1)}, u32[]{:S(2)}) copy-start(bf16[2,12,128,128]{3,0,1,2:T(2,128)(2,1)} %copy-done.1) | copy-start | bytes 2359300
  97.5 0.9 copy-start.3
  100.1 15.1 %all-to-all-start.6 = ((bf16[2,12,128,128]{3,0,1,2:T(2,128)(2,1)}), bf16[2,12,128,128]{3,0,1,2:T(2,128)(2,1)S(1)}, u32[]{:S(2)}, u32[]{:S(2)}) async-start(bf16[2,12,128,128]{3,0,1,2:T(2,128)(2,1)} %copy.217), calls=%async_computation.6 | async-start | bytes 1572864 | tf_op jit(solution)/shard_map/all_to_all | solution.py:82
  115.2 15.8 %all-to-all-start.5 = ((bf16[2,12,128,128]{3,0,1,2:T(2,128)(2,1)}), bf16[2,12,128,128]{3,0,1,2:T(2,128)(2,1)}, u32[]{:S(2)}, u32[]{:S(2)}) async-start(bf16[2,12,128,128]{3,0,1,2:T(2,128)(2,1)} %copy.213), calls=%async_computation.5 | async-start | bytes 1572864 | tf_op jit(solution)/shard_map/all_to_all | solution.py:81
  120.2 14.5 %copy-start.12 = (bf16[1024,2,128]{2,1,0:T(2,128)(2,1)S(1)}, bf16[1024,2,128]{2,1,0:T(2,128)(2,1)}, u32[]{:S(2)}) copy-start(bf16[1024,2,128]{2,1,0:T(2,128)(2,1)} %param.9) | copy-start | bytes 1572868
  131.0 15.1 %all-to-all-start.7 = ((bf16[2,12,128,128]{3,0,1,2:T(2,128)(2,1)}), bf16[2,12,128,128]{3,0,1,2:T(2,128)(2,1)S(1)}, u32[]{:S(2)}, u32[]{:S(2)}) async-start(bf16[2,12,128,128]{3,0,1,2:T(2,128)(2,1)} %copy.221), calls=%async_computation.7 | async-start | bytes 1572864 | tf_op jit(solution)/shard_map/all_to_all | solution.py:83
  134.6 89.2 %all-reduce.3.cloned.1.call-start = ((), (), s32[]{:S(2)}) async-start(), calls=%async_computation.10 | async-start | bytes 196608
  135.9 92.6 %reduce-scatter.2.cloned.1.call-start = ((), (), s32[]{:S(2)}) async-start(), calls=%async_computation.9 | async-start | bytes 4718592 | tf_op jit(solution)/shard_map/reduce_scatter | solution.py:95
  148.8 1.3 copy-start.5
  150.1 1.3 copy-start.6
  154.8 0.7 copy-start.13
Sparse Core Ops, SparseCore 0:
  139.3 84.5 all-reduce.2
Sparse Core Ops, SparseCore 1:
  154.9 36.9 reduce-scatter.1
where the time goes:
time: 239 us; the launch traced here: 238 us
  waiting for transfers between devices  121 us (51%)
  matrix products  35.6 us (15%)
  starting transfers between devices  35.5 us (15%)
  local copies, waits for them, and re-layouts  26.1 us (11%)
  between operations  16.6 us (7%)
  other arithmetic  3.23 us (1%)
    unnamed x3, waiting for transfers between devices  67.2 us
    all_to_all x1, waiting for transfers between devices, shards(): lax.all_to_all(pack(queries), 'seq', split_axis=2, concat_axis=2, tiled=T...  9.73 us
    all_to_all x1, waiting for transfers between devices, shards(): lax.all_to_all(grad_q, 'seq', split_axis=2, concat_axis=2, tiled=True)  9.14 us
    dot_general x4, matrix products, pack(): jnp.einsum('hst,thd->hsd', placing, tensor, preferred_element_type=jnp.fl...  9.09 us
    all_to_all x1, waiting for transfers between devices, shards(): lax.all_to_all(pack(keys), 'seq', split_axis=2, concat_axis=2, tiled=True)  8.58 us
    unnamed x34, local copies, waits for them, and re-layouts  7.94 us
    all_to_all x1, waiting for transfers between devices, shards(): lax.all_to_all(grad_k, 'seq', split_axis=2, concat_axis=2, tiled=True)  7.92 us
    dot_general x3, matrix products, unpack(): jnp.einsum('hst,hsd->thd', placing, rows, preferred_element_type=jnp.floa...  7.44 us
  transfers between devices with their start and end apart: 10, of which 9 were waited for; matrix products, arithmetic and copies ran while one was open for 21% of the time, Pallas kernels for 0%

commit v1 on v0

v1 whole, which is shorter than its diff:
```python
import math

import jax
import jax.numpy as jnp
from jax import lax
from jax.experimental import pallas as pl
from jax.experimental.pallas import tpu as pltpu
from jax.sharding import PartitionSpec as P

CLUSTERS = 192
SLOTS = 8
WIDTH = 128
TOK = 1024
SEQ = 16
CL_DEV = CLUSTERS // SEQ
ROWS = CLUSTERS * SLOTS
EMPTY = 1024.0
LIMIT = 100.0
VMEM = 56 * 1024 * 1024

f32 = jnp.float32
bf16 = jnp.bfloat16


def dot(a, b):
    return jnp.dot(a, b, preferred_element_type=f32)


def dot_nt(a, b):
    return lax.dot_general(a, b, (((1,), (1,)), ((), ())), preferred_element_type=f32)


def dot_tn(a, b):
    return lax.dot_general(a, b, (((0,), (0,)), ((), ())), preferred_element_type=f32)


def iota(shape, axis):
    return lax.broadcasted_iota(jnp.int32, shape, axis)


def pack_kernel(ids_ref, q_ref, k_ref, v_ref, g_ref, out_ref, flat_ref, rows_ref):
    i, j = iota((256, 256), 0), iota((256, 256), 1)
    split = (j == jnp.where(i < 128, 2 * i, 2 * i - 255)).astype(f32).astype(bf16)
    for b in range(TOK // 128):
        block = jnp.concatenate(
            [ref[256 * b : 256 * (b + 1), :] for ref in (q_ref, k_ref, v_ref, g_ref)], axis=1
        )
        parted = dot(split, block).astype(bf16)
        rows_ref[0, 128 * b : 128 * (b + 1), :] = parted[:128]
        rows_ref[1, 128 * b : 128 * (b + 1), :] = parted[128:]
    u, t = iota((256, 512), 0), iota((256, 512), 1)
    earlier = ((u < t) | (t >= 256)).astype(f32).astype(bf16)
    flats = []
    for h in range(2):
        ids = ids_ref[h]
        member = iota((CLUSTERS, TOK), 0) == ids
        member_b = member.astype(f32).astype(bf16)
        carry = jnp.zeros((CLUSTERS, 256), f32)
        ranks = []
        for b in range(TOK // 256):
            sums = dot(member_b[:, 256 * b : 256 * (b + 1)], earlier)
            before = sums[:, :256] + carry
            carry = carry + sums[:, 256:]
            mine = jnp.where(member[:, 256 * b : 256 * (b + 1)], before, 0.0)
            ranks.append(jnp.sum(mine, axis=0, keepdims=True))
        flat = ids * SLOTS + jnp.concatenate(ranks, axis=1).astype(jnp.int32)
        flat_ref[h] = flat
        flats.append(flat)
    dsts = 2
    step = dsts * CL_DEV * SLOTS
    slot = iota((step, TOK), 0)
    for j in range(SEQ // dsts):
        parts = []
        for h in range(2):
            place = (slot == flats[h] - j * step).astype(f32)
            used = jnp.sum(place, axis=1, keepdims=True) > 0.0
            moved = dot(place.astype(bf16), rows_ref[h])
            parts.append((moved, used))
        for x in range(4):
            halves = []
            for moved, used in parts:
                piece = moved[:, WIDTH * x : WIDTH * (x + 1)]
                if x == 1:
                    piece = jnp.where(used, piece, EMPTY)
                halves.append(piece.reshape(dsts * CL_DEV, SLOTS, WIDTH))
            tile = jnp.concatenate(halves, axis=1).astype(bf16)
            out_ref[dsts * j : dsts * (j + 1), x] = tile.reshape(dsts, CL_DEV, 2 * SLOTS, WIDTH)


def pack(ids, q, k, v, g):
    return pl.pallas_call(
        pack_kernel,
        out_shape=(
            jax.ShapeDtypeStruct((SEQ, 4, CL_DEV, 2 * SLOTS, WIDTH), bf16),
            jax.ShapeDtypeStruct((2, 1, TOK), jnp.int32),
        ),
        scratch_shapes=[pltpu.VMEM((2, TOK, 4 * WIDTH), bf16)],
        compiler_params=pltpu.CompilerParams(vmem_limit_bytes=VMEM),
        name="pack",
    )(ids, q, k, v, g)


PER_STEP = 4


def attend_kernel(in_ref, out_ref, sums_ref):
    scale = 1.0 / math.sqrt(WIDTH)
    count = SEQ * SLOTS
    key, query = iota((count, count), 0), iota((count, count), 1)
    causal, diagonal = key < query, key == query
    items = []
    for c in range(PER_STEP):
        wide = [in_ref[:, x, c].astype(f32) for x in range(4)]
        for h in range(2):
            items.append(
                [w[:, SLOTS * h : SLOTS * (h + 1)].reshape(count, WIDTH) for w in wide]
            )
    sums, grads = [], []
    for q32, k32, v32, g32 in items:
        q, k, v, g = (x.astype(bf16) for x in (q32, k32, v32, g32))
        empty = k32 > LIMIT
        sums.append(jnp.sum(jnp.where(empty, 0.0, k32), axis=0, keepdims=True))
        allowed = (causal & jnp.logical_not(empty)) | diagonal
        score = jnp.where(allowed, dot_nt(k, q) * scale, -1e30)
        dprob = dot_nt(v, g)
        top = jnp.max(score, axis=0, keepdims=True)
        expo = jnp.exp(score - top)
        prob = expo / jnp.sum(expo, axis=0, keepdims=True)
        prob_b = prob.astype(bf16)
        delta = jnp.sum(prob_b.astype(f32) * dprob, axis=0, keepdims=True)
        dscore = (prob * (dprob - delta) * scale).astype(bf16)
        grads.append((dot_tn(dscore, k), dot(dscore, q), dot(prob_b, g)))
    for c in range(PER_STEP):
        for x in range(3):
            halves = [grads[2 * c + h][x].reshape(SEQ, SLOTS, WIDTH) for h in range(2)]
            out_ref[:, x, c] = jnp.concatenate(halves, axis=1).astype(bf16)
    sums_ref[0] = jnp.concatenate(sums, axis=0) * scale


def attend(got):
    steps = CL_DEV // PER_STEP
    return pl.pallas_call(
        attend_kernel,
        grid=(steps,),
        in_specs=[
            pl.BlockSpec((SEQ, 4, PER_STEP, 2 * SLOTS, WIDTH), lambda i: (0, 0, i, 0, 0)),
        ],
        out_specs=(
            pl.BlockSpec((SEQ, 3, PER_STEP, 2 * SLOTS, WIDTH), lambda i: (0, 0, i, 0, 0)),
            pl.BlockSpec((1, 2 * PER_STEP, WIDTH), lambda i: (i, 0, 0)),
        ),
        out_shape=(
            jax.ShapeDtypeStruct((SEQ, 3, CL_DEV, 2 * SLOTS, WIDTH), bf16),
            jax.ShapeDtypeStruct((steps, 2 * PER_STEP, WIDTH), f32),
        ),
        compiler_params=pltpu.CompilerParams(vmem_limit_bytes=VMEM),
        name="attend",
    )(got)


def unpack_kernel(flat_ref, in_ref, q_ref, k_ref, v_ref, all_ref, rows_ref):
    for x in range(3):
        wide = in_ref[:, x].astype(f32)
        for h in range(2):
            part = wide[:, :, SLOTS * h : SLOTS * (h + 1)].reshape(ROWS, WIDTH)
            rows_ref[h, :, WIDTH * x : WIDTH * (x + 1)] = part.astype(bf16)
    columns = []
    for h in range(2):
        line = jnp.broadcast_to(flat_ref[h].astype(f32), (8, TOK))
        columns.append(line.T[:, :1].astype(jnp.int32))
    i, j = iota((256, 256), 0), iota((256, 256), 1)
    merge = (i == jnp.where(j < 128, 2 * j, 2 * j - 255)).astype(f32).astype(bf16)
    slot = iota((256, ROWS), 1)
    for b in range(TOK // 256):
        found = []
        for h in range(2):
            place = (slot == columns[h][256 * b : 256 * (b + 1)]).astype(f32).astype(bf16)
            rows = dot(place, rows_ref[h]).astype(bf16)
            all_ref[256 * b : 256 * (b + 1), 384 * h : 384 * (h + 1)] = rows
            found.append(rows)
        for s in range(2):
            both = jnp.concatenate([rows[128 * s : 128 * (s + 1)] for rows in found], axis=0)
            mixed = dot(merge, both).astype(bf16)
            at = 512 * b + 256 * s
            q_ref[at : at + 256, :] = mixed[:, :128]
            k_ref[at : at + 256, :] = mixed[:, 128:256]
            v_ref[at : at + 256, :] = mixed[:, 256:]


def unpack(flat, got):
    one = jax.ShapeDtypeStruct((2 * TOK, WIDTH), bf16)
    return pl.pallas_call(
        unpack_kernel,
        out_shape=(one, one, one, jax.ShapeDtypeStruct((TOK, 6 * WIDTH), bf16)),
        scratch_shapes=[pltpu.VMEM((2, ROWS, 3 * WIDTH), bf16)],
        compiler_params=pltpu.CompilerParams(vmem_limit_bytes=VMEM),
        name="unpack",
    )(flat, got)


def shards(queries, keys, values, out_grad, cluster_ids, query_weight, key_weight, value_weight):
    place = lax.axis_index("head")
    core, z = place % 2, place // 2
    swap = [(i, i ^ 1) for i in range(8)]
    up = [(i, (i + 2) % 8) for i in range(8)]
    down = [(i, (i - 2) % 8) for i in range(8)]

    def blocks(which):
        parts = [w.reshape(4, 2, 256, 2, WIDTH) for w in (query_weight, key_weight, value_weight)]
        parts = [lax.dynamic_index_in_dim(w, which, 1, keepdims=False) for w in parts]
        whole = jnp.stack(parts, axis=3).reshape(4, 256, 6 * WIDTH)
        return jnp.roll(whole, -z, axis=0)

    weight_own = blocks(core)
    weight_other = lax.ppermute(blocks(1 - core), "head", swap)

    ids = jnp.transpose(cluster_ids, (0, 2, 1))
    flat2 = [x.reshape(2 * TOK, WIDTH) for x in (queries, keys, values, out_grad)]
    sent, flat = pack(ids, *flat2)
    got = lax.all_to_all(sent, "seq", split_axis=0, concat_axis=0, tiled=True)
    back, sums = attend(got)
    key_sums = jnp.transpose(sums.reshape(CL_DEV, 2, WIDTH), (1, 0, 2))
    home = lax.all_to_all(back, "seq", split_axis=0, concat_axis=0, tiled=True)
    grad_q, grad_k, grad_v, own = unpack(flat, home)
    other = lax.ppermute(own, "head", swap)

    def part(j, lo=0, hi=256):
        return dot_nt(weight_own[j, lo:hi], own) + dot_nt(weight_other[j, lo:hi], other)

    far = part(2).astype(bf16)
    up_far = lax.ppermute(far[:128], "head", up)
    down_far = lax.ppermute(far[128:], "head", down)
    up_near = lax.ppermute(part(1, 128, 256).astype(bf16), "head", up)
    down_near = lax.ppermute(part(3, 0, 128).astype(bf16), "head", down)
    up_sum = lax.ppermute((part(1, 0, 128) + up_far.astype(f32)).astype(bf16), "head", up)
    down_sum = lax.ppermute((part(3, 128, 256) + down_far.astype(f32)).astype(bf16), "head", down)
    mine = part(0)
    first = mine[:128] + up_sum.astype(f32) + down_near.astype(f32)
    last = mine[128:] + up_near.astype(f32) + down_sum.astype(f32)
    input_grad = jnp.concatenate([first, last], axis=0).astype(bf16)
    grads = [x.reshape(TOK, 2, WIDTH) for x in (grad_q, grad_k, grad_v)]
    return (*grads, input_grad, key_sums)


def solution(mesh):
    placed = (
        P("seq", "head", None),
        P("seq", "head", None),
        P("seq", "head", None),
        P("seq", "head", None),
        P("head", "seq", None),
        P(None, "head", None),
        P(None, "head", None),
        P(None, "head", None),
    )
    return jax.shard_map(
        shards,
        mesh=mesh,
        in_specs=placed,
        out_specs=(
            P("seq", "head", None),
            P("seq", "head", None),
            P("seq", "head", None),
            P("head", "seq"),
            P("head", "seq", None),
        ),
        check_vma=False,
    )
```

time: 239 us -> 147 us (0.62)
  waiting for transfers between devices: 121 us -> 17.6 us
  blocking collectives: 0 us -> 46.7 us
  Pallas kernels: 0 us -> 26.6 us
  matrix products: 35.6 us -> 14.9 us
  starting transfers between devices: 35.5 us -> 15.1 us
  between operations: 16.6 us -> 0.89 us
  local copies, waits for them, and re-layouts: 26.1 us -> 17.7 us
  other arithmetic: 3.23 us -> 7.35 us
    unnamed x3 -> x0, waiting for transfers between devices: 67.2 us -> none
    all_to_all x0 -> x1, blocking collectives: none -> 46.7 us  [shards(): got = lax.all_to_all(sent, 'seq', split_axis=0, concat_axis=0, tiled=True)]
    all_to_all x8 -> x1, waiting for transfers between devices: 53.7 us -> 9 us  [shards(): home = lax.all_to_all(back, 'seq', split_axis=0, concat_axis=0, tiled=True)]
    all_to_all x8 -> x1, starting transfers between devices: 35.2 us -> 4.03 us  [shards(): home = lax.all_to_all(back, 'seq', split_axis=0, concat_axis=0, tiled=True)]
    pallas_call x0 -> x3, Pallas kernels: none -> 26.6 us  [the longest x1 9.61 us: pack(): pl.pallas_call(pack_kernel, out_shape=(jax.ShapeDtypeStruct((SEQ, 4, CL_D...]
    dot_general x16 -> x12, matrix products: 29.3 us -> 14.9 us  [dot_nt(): lax.dot_general(a, b, (((1,), (1,)), ((), ())), preferred_element_type=f32)]
    ppermute x0 -> x8, starting transfers between devices: none -> 11 us  [the longest x1 3.41 us: shards(): lax.ppermute((part(3, 128, 256) + down_far.astype(f32)).astype(bf16), 'he...]
    ppermute x0 -> x8, waiting for transfers between devices: none -> 8.6 us  [the longest x1 4.24 us: shards(): lax.ppermute((part(1, 0, 128) + up_far.astype(f32)).astype(bf16), 'head',...]
  transfers between devices with their start and end apart: 10 -> 9, of which waited for: 9 -> 4; matrix products, arithmetic and copies ran while one was open for 21% -> 24% of each run, Pallas kernels for 0% -> 6%
where the time goes in v1:
time: 147 us
  blocking collectives  46.7 us (32%)
  Pallas kernels  26.6 us (18%)
  local copies, waits for them, and re-layouts  17.7 us (12%)
  waiting for transfers between devices  17.6 us (12%)
  starting transfers between devices  15.1 us (10%)
  matrix products  14.9 us (10%)
  other arithmetic  7.35 us (5%)
    all_to_all x1, blocking collectives, shards(): got = lax.all_to_all(sent, 'seq', split_axis=0, concat_axis=0, tiled=True)  46.7 us
    dot_general x12, matrix products, dot_nt(): lax.dot_general(a, b, (((1,), (1,)), ((), ())), preferred_element_type=f32)  14.9 us
    unnamed x14, local copies, waits for them, and re-layouts  10.7 us
    pallas_call x1, Pallas kernels, pack(): pl.pallas_call(pack_kernel, out_shape=(jax.ShapeDtypeStruct((SEQ, 4, CL_D...  9.61 us
    all_to_all x1, waiting for transfers between devices, shards(): home = lax.all_to_all(back, 'seq', split_axis=0, concat_axis=0, tiled=True)  9 us
    pallas_call x1, Pallas kernels, attend(): pl.pallas_call(attend_kernel, grid=(steps,), in_specs=[pl.BlockSpec((SEQ,...  8.94 us
    pallas_call x1, Pallas kernels, unpack(): pl.pallas_call(unpack_kernel, out_shape=(one, one, one, jax.ShapeDtypeStr...  8.09 us
    dynamic_slice x2, local copies, waits for them, and re-layouts, blocks(): lax.dynamic_index_in_dim(w, which, 1, keepdims=False)  6.92 us
  transfers between devices with their start and end apart: 9, of which 4 were waited for; matrix products, arithmetic and copies ran while one was open for 24% of the time, Pallas kernels for 6%

profile of v1, /device:TPU:0, one launch (start us, length us, event | category | flops | bytes accessed | tf_op | source)
XLA Modules:
  0.0 146.8 jit_solution(6892039186984795053)
XLA Ops:
  0.6 9.6 %pack.1 = (bf16[16,4,12,16,128]{4,3,2,1,0:T(8,128)(2,1)}, s32[2,1,1024]{2,1,0:T(1,128)}) custom-call(s32[2,1,1024]{2,1,0:T(1,128)} %bitcast.85, bf16[2048,128]{1,0:T(8,128)(2,1)} %bitcast.81, bf16[2048,128]{1,0:T(8,128)(2,1)} %bitcast.82, bf16[2048,128]{1,0:T(8,128)(2,1)} %bitcast.83, bf16[2048,128]{1,0:T(8,128)(2,1)} %bitcast.84), custom_call_target="tpu_custom_call" | custom-call | tf_op jit(solution)/shard_map/pack/pallas_call | solution.py:91
  10.2 46.7 %all_to_all.10.in_ref = bf16[16,4,12,16,128]{4,3,2,1,0:T(8,128)(2,1)} all-to-all(bf16[16,4,12,16,128]{4,3,2,1,0:T(8,128)(2,1)} %get-tuple-element.15), channel_id=1, replica_groups=mesh['head'=8,'seq'=16] {'seq'}, dimensions={0} | all-to-all | bytes 6291456 | tf_op jit(solution)/shard_map/all_to_all | solution.py:220
  56.9 8.9 %attend.1 = (bf16[16,3,12,16,128]{4,3,2,1,0:T(8,128)(2,1)}, f32[3,8,128]{2,1,0:T(8,128)}) custom-call(bf16[16,4,12,16,128]{4,3,2,1,0:T(8,128)(2,1)} %all_to_all.10.in_ref), custom_call_target="tpu_custom_call" | custom-call | tf_op jit(solution)/shard_map/attend/pallas_call | solution.py:142
  65.9 4.0 %all-to-all-start.1 = ((bf16[16,3,12,16,128]{4,3,2,1,0:T(8,128)(2,1)}), bf16[16,3,12,16,128]{4,3,2,1,0:T(8,128)(2,1)S(1)}, u32[]{:S(2)}, u32[]{:S(2)}) async-start(bf16[16,3,12,16,128]{4,3,2,1,0:T(8,128)(2,1)} %get-tuple-element.16), calls=%async_computation.1 | async-start | bytes 4718592 | tf_op jit(solution)/shard_map/all_to_all | solution.py:223
  70.0 4.0 %constant_dynamic-slice_fusion = (bf16[4,1,256,2,128]{4,3,2,1,0:T(2,128)(2,1)}, bf16[4,1,256,2,128]{4,3,2,1,0:T(2,128)(2,1)S(1)}, bf16[4,1,256,2,128]{4,3,2,1,0:T(2,128)(2,1)S(1)}, bf16[4,1,256,2,128]{4,3,2,1,0:T(2,128)(2,1)}) fusion(bf16[4,2,256,2,128]{4,3,2,1,0:T(2,128)(2,1)} %bitcast.78, s32[]{:T(128)S(6)} %select_n.34, s32[]{:T(128)S(6)} %select_n.32, ...), kind=kLoop, calls=%fused_computation.46 | loop fusion | bytes 4194312 | tf_op jit(solution)/shard_map/jit(dynamic_index_in_dim)/dynamic_slice | solution.py:210
  74.0 2.0 %copy.23 = bf16[4,1,256,2,128]{2,4,3,0,1:T(8,128)(2,1)} copy(bf16[4,1,256,2,128]{4,3,2,1,0:T(2,128)(2,1)} %get-tuple-element.33) | data formatting | bytes 1048576
  76.0 2.0 %copy.24 = bf16[4,1,256,2,128]{2,4,3,0,1:T(8,128)(2,1)} copy(bf16[4,1,256,2,128]{4,3,2,1,0:T(2,128)(2,1)} %get-tuple-element.28) | data formatting | bytes 1048576
  77.9 2.9 %constant_dynamic-slice_fusion.2 = (bf16[4,1,256,2,128]{4,3,2,1,0:T(2,128)(2,1)}, bf16[4,1,256,2,128]{4,3,2,1,0:T(2,128)(2,1)}) fusion(bf16[4,2,256,2,128]{4,3,2,1,0:T(2,128)(2,1)} %bitcast.80, s32[]{:T(128)S(6)} %select_n.34, s32[]{:T(128)S(6)} %select_n.32), kind=kLoop, calls=%fused_computation.48 | loop fusion | bytes 2097160 | tf_op jit(solution)/shard_map/jit(dynamic_index_in_dim)/dynamic_slice | solution.py:210
  80.8 2.0 %copy.22 = bf16[4,1,256,2,128]{2,4,3,0,1:T(8,128)(2,1)} copy(bf16[4,1,256,2,128]{4,3,2,1,0:T(2,128)(2,1)} %get-tuple-element.24) | data formatting | bytes 1048576
  82.8 1.5 %pad_maximum_fusion.1 = bf16[4,256,2,3,128]{1,4,3,2,0:T(8,128)(2,1)S(1)} fusion(bf16[4,256,2,1,128]{1,4,3,2,0:T(8,128)(2,1)} %bitcast.73, bf16[4,256,2,1,128]{1,4,3,2,0:T(8,128)(2,1)} %bitcast.72, bf16[4,256,2,1,128]{1,4,3,2,0:T(8,128)(2,1)} %bitcast.74), kind=kLoop, calls=%fused_computation.7 | loop fusion | flops 1572864 | bytes 3145728 | tf_op jit(solution)/shard_map/stack | solution.py:211
  84.3 1.8 %fusion = bf16[4,256,768]{1,2,0:T(8,128)(2,1)} fusion(s32[]{:T(128)S(6)} %select_n.38, bf16[4,256,768]{1,2,0:T(8,128)(2,1)S(1)} %bitcast.71), kind=kLoop, calls=%fused_computation.4 | loop fusion | flops 786432 | bytes 3145732 | tf_op jit(solution)/shard_map/jit(_roll_dynamic)/concatenate | solution.py:212
  86.1 1.1 copy.20
  88.2 1.3 copy.19
  89.5 1.2 pad_maximum_fusion
  90.7 1.8 %fusion.1 = bf16[4,256,768]{1,2,0:T(8,128)(2,1)} fusion(s32[]{:T(128)S(6)} %select_n.38, bf16[4,256,768]{1,2,0:T(8,128)(2,1)S(1)} %bitcast.70), kind=kLoop, calls=%fused_computation.5 | loop fusion | flops 786432 | bytes 3145732 | tf_op jit(solution)/shard_map/jit(_roll_dynamic)/concatenate | solution.py:212
  92.5 9.0 %all-to-all-done.1.in_ref = bf16[16,3,12,16,128]{4,3,2,1,0:T(8,128)(2,1)S(1)} async-done(((bf16[16,3,12,16,128]{4,3,2,1,0:T(8,128)(2,1)}), bf16[16,3,12,16,128]{4,3,2,1,0:T(8,128)(2,1)S(1)}, u32[]{:S(2)}, u32[]{:S(2)}) %all-to-all-start.1) | async-done | bytes 2359328 | tf_op jit(solution)/shard_map/all_to_all | solution.py:223
  101.5 1.4 copy-done.1
  102.9 8.1 %unpack.1 = (bf16[2048,128]{1,0:T(8,128)(2,1)}, bf16[2048,128]{1,0:T(8,128)(2,1)}, bf16[2048,128]{1,0:T(8,128)(2,1)}, bf16[1024,768]{1,0:T(8,128)(2,1)}) custom-call(s32[2,1,1024]{2,1,0:T(1,128)} %get-tuple-element.14.flat_ref, bf16[16,3,12,16,128]{4,3,2,1,0:T(8,128)(2,1)} %copy-done.1), custom_call_target="tpu_custom_call" | custom-call | tf_op jit(solution)/shard_map/unpack/pallas_call | solution.py:192
  111.0 2.2 %fusion.16 = f32[128,1024]{1,0:T(8,128)S(1)} fusion(bf16[1024,768]{1,0:T(8,128)(2,1)} %get-tuple-element.20, bf16[4,256,768]{1,2,0:T(8,128)(2,1)S(1)} %copy-done.2), kind=kOutput, calls=%fused_computation.39 | convolution fusion | flops 201326592 | bytes 2293760 | tf_op jit(solution)/shard_map/dot_general | solution.py:30
  116.4 1.6 %fusion.7 = bf16[128,1024]{1,0:T(8,128)(2,1)S(1)} fusion(f32[128,1024]{1,0:T(8,128)S(1)} %fusion.16, bf16[1024,768]{1,0:T(8,128)(2,1)S(1)} %collective-permute-done.1, bf16[4,256,768]{1,2,0:T(8,128)(2,1)} %collective-permute-done), kind=kOutput, calls=%fused_computation.19 | convolution fusion | flops 201588736 | bytes 2555904 | tf_op jit(solution)/shard_map/dot_general | solution.py:30
  118.0 2.0 %collective-permute-start.5 = (bf16[128,1024]{1,0:T(8,128)(2,1)S(1)}, bf16[128,1024]{1,0:T(8,128)(2,1)S(1)}, u32[]{:S(2)}, u32[]{:S(2)}) collective-permute-start(bf16[128,1024]{1,0:T(8,128)(2,1)S(1)} %fusion.7), channel_id=1, source_target_pairs={{0,32},{16,48},{32,64},{48,80},{64,96},{80,112},{96,0},{112,16},{1... | collective-permute-start | bytes 786440 | tf_op jit(solution)/shard_map/ppermute | solution.py:233
  120.0 1.6 %fusion.2 = bf16[256,1024]{1,0:T(8,128)(2,1)S(1)} fusion(f32[256,1024]{1,0:T(8,128)S(1)} %fusion.13, bf16[1024,768]{1,0:T(8,128)(2,1)S(1)} %collective-permute-done.1, bf16[4,256,768]{1,2,0:T(8,128)(2,1)} %collective-permute-done), kind=kOutput, calls=%fused_computation.10 | convolution fusion | flops 403177472 | bytes 3538944 | tf_op jit(solution)/shard_map/dot_general | solution.py:30
  121.7 2.2 %collective-permute-start.6 = (bf16[128,1024]{1,0:T(8,128)(2,1)S(1)}, bf16[128,1024]{1,0:T(8,128)(2,1)S(1)}, u32[]{:S(2)}, u32[]{:S(2)}) collective-permute-start(bf16[128,1024]{1,0:T(8,128)(2,1)S(1)} %get-tuple-element.31), channel_id=1, source_target_pairs={{0,96},{16,112},{32,0},{48,16},{64,32},{80,48},{96,64},{112,80},{1... | collective-permute-start | bytes 786440 | tf_op jit(solution)/shard_map/ppermute | solution.py:232
  123.9 1.6 %fusion.6 = bf16[128,1024]{1,0:T(8,128)(2,1)S(1)} fusion(f32[128,1024]{1,0:T(8,128)S(1)} %fusion.17, bf16[1024,768]{1,0:T(8,128)(2,1)S(1)} %collective-permute-done.1, bf16[4,256,768]{1,2,0:T(8,128)(2,1)} %collective-permute-done), kind=kOutput, calls=%fused_computation.18 | convolution fusion | flops 201588736 | bytes 2555904 | tf_op jit(solution)/shard_map/dot_general | solution.py:30
  125.5 3.3 %collective-permute-start.4 = (bf16[128,1024]{1,0:T(8,128)(2,1)S(1)}, bf16[128,1024]{1,0:T(8,128)(2,1)S(1)}, u32[]{:S(2)}, u32[]{:S(2)}) collective-permute-start(bf16[128,1024]{1,0:T(8,128)(2,1)S(1)} %fusion.6), channel_id=1, source_target_pairs={{0,96},{16,112},{32,0},{48,16},{64,32},{80,48},{96,64},{112,80},{1... | collective-permute-start | bytes 786440 | tf_op jit(solution)/shard_map/ppermute | solution.py:234
  128.8 2.1 %collective-permute-done.6 = bf16[128,1024]{1,0:T(8,128)(2,1)S(1)} collective-permute-done((bf16[128,1024]{1,0:T(8,128)(2,1)S(1)}, bf16[128,1024]{1,0:T(8,128)(2,1)S(1)}, u32[]{:S(2)}, u32[]{:S(2)}) %collective-permute-start.6) | collective-permute-done | bytes 262176 | tf_op jit(solution)/shard_map/ppermute | solution.py:232
  130.9 1.6 %fusion.8 = bf16[128,1024]{1,0:T(8,128)(2,1)S(1)} fusion(f32[128,1024]{1,0:T(8,128)S(1)} %fusion.15, bf16[1024,768]{1,0:T(8,128)(2,1)S(1)} %collective-permute-done.1, bf16[128,1024]{1,0:T(8,128)(2,1)S(1)} %collective-permute-done.6, bf16[4,256,768]{1,2,0:T(8,128)(2,1)} %collective-permute-done), kind=kOutput, calls=%fused_computation.20 | convolution fusion | flops 201850880 | bytes 2818048 | tf_op jit(solution)/shard_map/dot_general | solution.py:30
  132.5 3.4 %collective-permute-start.7 = (bf16[128,1024]{1,0:T(8,128)(2,1)S(1)}, bf16[128,1024]{1,0:T(8,128)(2,1)S(1)}, u32[]{:S(2)}, u32[]{:S(2)}) collective-permute-start(bf16[128,1024]{1,0:T(8,128)(2,1)S(1)} %fusion.8), channel_id=1, source_target_pairs={{0,96},{16,112},{32,0},{48,16},{64,32},{80,48},{96,64},{112,80},{1... | collective-permute-start | bytes 786440 | tf_op jit(solution)/shard_map/ppermute | solution.py:236
  135.9 1.6 %fusion.5 = bf16[128,1024]{1,0:T(8,128)(2,1)S(1)} fusion(f32[128,1024]{1,0:T(8,128)S(1)} %fusion.18, bf16[1024,768]{1,0:T(8,128)(2,1)S(1)} %collective-permute-done.1, bf16[128,1024]{1,0:T(8,128)(2,1)S(1)} %collective-permute-done.2, bf16[4,256,768]{1,2,0:T(8,128)(2,1)} %collective-permute-done), kind=kOutput, calls=%fused_computation.17 | convolution fusion | flops 201850880 | bytes 2818048 | tf_op jit(solution)/shard_map/dot_general | solution.py:30
  137.6 1.6 %convolution_add_fusion.1 = f32[256,1024]{1,0:T(8,128)S(1)} fusion(f32[256,1024]{1,0:T(8,128)S(1)} %fusion.14, bf16[1024,768]{1,0:T(8,128)(2,1)S(1)} %collective-permute-done.1, bf16[4,256,768]{1,2,0:T(8,128)(2,1)} %collective-permute-done), kind=kOutput, calls=%fused_computation.9 | convolution fusion | flops 402915328 | bytes 4063232 | tf_op jit(solution)/shard_map/dot_general | solution.py:30
  139.2 2.2 %collective-permute-done.7 = bf16[128,1024]{1,0:T(8,128)(2,1)S(1)} collective-permute-done((bf16[128,1024]{1,0:T(8,128)(2,1)S(1)}, bf16[128,1024]{1,0:T(8,128)(2,1)S(1)}, u32[]{:S(2)}, u32[]{:S(2)}) %collective-permute-start.7) | collective-permute-done | bytes 262176 | tf_op jit(solution)/shard_map/ppermute | solution.py:236
  141.5 4.2 %collective-permute-done.3 = bf16[128,1024]{1,0:T(8,128)(2,1)S(1)} collective-permute-done((bf16[128,1024]{1,0:T(8,128)(2,1)S(1)}, bf16[128,1024]{1,0:T(8,128)(2,1)S(1)}, u32[]{:S(2)}, u32[]{:S(2)}) %collective-permute-start.3) | collective-permute-done | bytes 262176 | tf_op jit(solution)/shard_map/ppermute | solution.py:235
  (25 shorter events, 5.4 us)
Async XLA Ops:
  65.9 35.6 %all-to-all-start.1 = ((bf16[16,3,12,16,128]{4,3,2,1,0:T(8,128)(2,1)}), bf16[16,3,12,16,128]{4,3,2,1,0:T(8,128)(2,1)S(1)}, u32[]{:S(2)}, u32[]{:S(2)}) async-start(bf16[16,3,12,16,128]{4,3,2,1,0:T(8,128)(2,1)} %get-tuple-element.16), calls=%async_computation.1 | async-start | bytes 4718592 | tf_op jit(solution)/shard_map/all_to_all | solution.py:223
  86.1 30.3 %collective-permute-start = (bf16[4,256,768]{1,2,0:T(8,128)(2,1)}, bf16[4,256,768]{1,2,0:T(8,128)(2,1)}, u32[]{:S(2)}, u32[]{:S(2)}) collective-permute-start(bf16[4,256,768]{1,2,0:T(8,128)(2,1)} %fusion), channel_id=1, source_target_pairs={{0,16},{16,0},{32,48},{48,32},{64,80},{80,64},{96,112},{112,96},{1... | collective-permute-start | bytes 4718600 | tf_op jit(solution)/shard_map/ppermute | solution.py:215
  87.1 2.3 %copy-start.3 = (bf16[4,1,256,2,128]{2,4,3,0,1:T(8,128)(2,1)S(1)}, bf16[4,1,256,2,128]{2,4,3,0,1:T(8,128)(2,1)}, u32[]{:S(2)}) copy-start(bf16[4,1,256,2,128]{2,4,3,0,1:T(8,128)(2,1)} %copy.20) | copy-start | bytes 1572868
  101.5 1.4 copy-start.1
  101.5 9.5 %copy-start.2 = (bf16[4,256,768]{1,2,0:T(8,128)(2,1)S(1)}, bf16[4,256,768]{1,2,0:T(8,128)(2,1)}, u32[]{:S(2)}) copy-start(bf16[4,256,768]{1,2,0:T(8,128)(2,1)} %fusion.1) | copy-start | bytes 4718596
  111.0 2.2 %copy-start = (bf16[1024,768]{1,0:T(8,128)(2,1)S(1)}, bf16[1024,768]{1,0:T(8,128)(2,1)}, u32[]{:S(2)}) copy-start(bf16[1024,768]{1,0:T(8,128)(2,1)} %get-tuple-element.20) | copy-start | bytes 4718596
  111.0 5.4 %collective-permute-start.1 = (bf16[1024,768]{1,0:T(8,128)(2,1)}, bf16[1024,768]{1,0:T(8,128)(2,1)S(1)}, u32[]{:S(2)}, u32[]{:S(2)}) collective-permute-start(bf16[1024,768]{1,0:T(8,128)(2,1)} %get-tuple-element.20), channel_id=1, source_target_pairs={{0,16},{16,0},{32,48},{48,32},{64,80},{80,64},{96,112},{112,96},{1... | collective-permute-start | bytes 4718600 | tf_op jit(solution)/shard_map/ppermute | solution.py:225
  118.0 21.2 %collective-permute-start.5 = (bf16[128,1024]{1,0:T(8,128)(2,1)S(1)}, bf16[128,1024]{1,0:T(8,128)(2,1)S(1)}, u32[]{:S(2)}, u32[]{:S(2)}) collective-permute-start(bf16[128,1024]{1,0:T(8,128)(2,1)S(1)} %fusion.7), channel_id=1, source_target_pairs={{0,32},{16,48},{32,64},{48,80},{64,96},{80,112},{96,0},{112,16},{1... | collective-permute-start | bytes 786440 | tf_op jit(solution)/shard_map/ppermute | solution.py:233
  121.7 9.2 %collective-permute-start.6 = (bf16[128,1024]{1,0:T(8,128)(2,1)S(1)}, bf16[128,1024]{1,0:T(8,128)(2,1)S(1)}, u32[]{:S(2)}, u32[]{:S(2)}) collective-permute-start(bf16[128,1024]{1,0:T(8,128)(2,1)S(1)} %get-tuple-element.31), channel_id=1, source_target_pairs={{0,96},{16,112},{32,0},{48,16},{64,32},{80,48},{96,64},{112,80},{1... | collective-permute-start | bytes 786440 | tf_op jit(solution)/shard_map/ppermute | solution.py:232
  123.9 12.0 %collective-permute-start.2 = (bf16[128,1024]{1,0:T(8,128)(2,1)S(1)}, bf16[128,1024]{1,0:T(8,128)(2,1)S(1)}, u32[]{:S(2)}, u32[]{:S(2)}) collective-permute-start(bf16[128,1024]{1,0:T(8,128)(2,1)S(1)} %get-tuple-element.30), channel_id=1, source_target_pairs={{0,32},{16,48},{32,64},{48,80},{64,96},{80,112},{96,0},{112,16},{1... | collective-permute-start | bytes 786440 | tf_op jit(solution)/shard_map/ppermute | solution.py:231
  125.5 13.7 %collective-permute-start.4 = (bf16[128,1024]{1,0:T(8,128)(2,1)S(1)}, bf16[128,1024]{1,0:T(8,128)(2,1)S(1)}, u32[]{:S(2)}, u32[]{:S(2)}) collective-permute-start(bf16[128,1024]{1,0:T(8,128)(2,1)S(1)} %fusion.6), channel_id=1, source_target_pairs={{0,96},{16,112},{32,0},{48,16},{64,32},{80,48},{96,64},{112,80},{1... | collective-permute-start | bytes 786440 | tf_op jit(solution)/shard_map/ppermute | solution.py:234
  132.5 9.0 %collective-permute-start.7 = (bf16[128,1024]{1,0:T(8,128)(2,1)S(1)}, bf16[128,1024]{1,0:T(8,128)(2,1)S(1)}, u32[]{:S(2)}, u32[]{:S(2)}) collective-permute-start(bf16[128,1024]{1,0:T(8,128)(2,1)S(1)} %fusion.8), channel_id=1, source_target_pairs={{0,96},{16,112},{32,0},{48,16},{64,32},{80,48},{96,64},{112,80},{1... | collective-permute-start | bytes 786440 | tf_op jit(solution)/shard_map/ppermute | solution.py:236
  137.5 8.2 %collective-permute-start.3 = (bf16[128,1024]{1,0:T(8,128)(2,1)S(1)}, bf16[128,1024]{1,0:T(8,128)(2,1)S(1)}, u32[]{:S(2)}, u32[]{:S(2)}) collective-permute-start(bf16[128,1024]{1,0:T(8,128)(2,1)S(1)} %fusion.5), channel_id=1, source_target_pairs={{0,32},{16,48},{32,64},{48,80},{64,96},{80,112},{96,0},{112,16},{1... | collective-permute-start | bytes 786440 | tf_op jit(solution)/shard_map/ppermute | solution.py:235

commit v2 on v1

v2 whole, which is shorter than its diff:
```python
import functools
import math

import jax
import jax.numpy as jnp
from jax import lax
from jax.experimental import pallas as pl
from jax.experimental.pallas import tpu as pltpu
from jax.sharding import PartitionSpec as P

CLUSTERS = 192
SLOTS = 8
WIDTH = 128
TOK = 1024
HALF = TOK // 2
SEQ = 16
CL_DEV = CLUSTERS // SEQ
RUN = CL_DEV * SLOTS
ROWS = CLUSTERS * SLOTS
QUARTER = 256
EMPTY = 1024.0
LIMIT = 100.0
PACK_DSTS = 2

f32 = jnp.float32
bf16 = jnp.bfloat16
WHOLE = pl.BlockSpec(memory_space=pltpu.VMEM)
MIB = 1024 * 1024


def near(x):
    return pltpu.with_memory_space_constraint(x, pltpu.VMEM)


def dot(a, b):
    return jnp.dot(a, b, preferred_element_type=f32)


def dot_nt(a, b):
    return lax.dot_general(a, b, (((1,), (1,)), ((), ())), preferred_element_type=f32)


def dot_tn(a, b):
    return lax.dot_general(a, b, (((0,), (0,)), ((), ())), preferred_element_type=f32)


def iota(shape, axis):
    return lax.broadcasted_iota(jnp.int32, shape, axis)


def pack_kernel(ids_ref, q_ref, k_ref, v_ref, g_ref, out_ref, flat_ref, pairs_ref, rows_ref, sem):
    copies = []
    for x, ref in enumerate((q_ref, k_ref, v_ref, g_ref)):
        copy = pltpu.make_async_copy(ref, pairs_ref.at[x], sem.at[x])
        copy.start()
        copies.append(copy)
    u, t = iota((256, 512), 0), iota((256, 512), 1)
    earlier = ((u < t) | (t >= 256)).astype(f32).astype(bf16)
    ids = [ids_ref[h] for h in range(2)]
    cluster = iota((CLUSTERS, 256), 0)
    carry = jnp.zeros((2 * CLUSTERS, 256), f32)
    ranks = [[], []]
    for b in range(TOK // 256):
        member = jnp.concatenate(
            [(cluster == line[:, 256 * b : 256 * (b + 1)]).astype(f32) for line in ids], axis=0
        )
        sums = dot(member.astype(bf16), earlier)
        mine = member * (sums[:, :256] + carry)
        carry = carry + sums[:, 256:]
        for h in range(2):
            part = mine[CLUSTERS * h : CLUSTERS * (h + 1)]
            ranks[h].append(jnp.sum(part, axis=0, keepdims=True))
    flats = []
    for h in range(2):
        flat = ids[h] * SLOTS + jnp.concatenate(ranks[h], axis=1).astype(jnp.int32)
        flat_ref[h] = flat
        flats.append(flat)
    for copy in copies:
        copy.wait()
    i, j = iota((256, 256), 0), iota((256, 256), 1)
    split = (j == jnp.where(i < 128, 2 * i, 2 * i - 255)).astype(f32).astype(bf16)
    for b in range(TOK // 128):
        block = jnp.concatenate([pairs_ref[x, 256 * b : 256 * (b + 1), :] for x in range(4)], axis=1)
        parted = dot(split, block).astype(bf16)
        rows_ref[0, 128 * b : 128 * (b + 1), :] = parted[:128]
        rows_ref[1, 128 * b : 128 * (b + 1), :] = parted[128:]
    step = PACK_DSTS * RUN
    slot = iota((step, TOK), 0)
    groups = (PACK_DSTS * CL_DEV, SLOTS, WIDTH)
    rank = iota(groups, 1).astype(f32)
    for j in range(SEQ // PACK_DSTS):
        for h in range(2):
            place = (slot == flats[h] - j * step).astype(f32).astype(bf16)
            moved = dot(place, rows_ref[h])
            for x in range(4):
                piece = moved[:, WIDTH * x : WIDTH * (x + 1)]
                if x == 1:
                    at = CLUSTERS * h + groups[0] * j
                    count = jnp.broadcast_to(carry[at : at + groups[0], None, :WIDTH], groups)
                    piece = jnp.where(rank < count, piece.reshape(groups), EMPTY)
                piece = piece.reshape(PACK_DSTS, RUN, WIDTH).astype(bf16)
                out_ref[PACK_DSTS * j : PACK_DSTS * (j + 1), x, h] = piece


def pack(ids, *tensors):
    far = [pltpu.with_memory_space_constraint(x, pltpu.HBM) for x in tensors]
    return pl.pallas_call(
        pack_kernel,
        in_specs=[WHOLE] + [pl.BlockSpec(memory_space=pltpu.HBM)] * 4,
        out_specs=(WHOLE, WHOLE),
        out_shape=(
            pltpu.VMEM((SEQ, 4, 2, RUN, WIDTH), bf16),
            jax.ShapeDtypeStruct((2, 1, TOK), jnp.int32),
        ),
        scratch_shapes=[
            pltpu.VMEM((4, 2 * TOK, WIDTH), bf16),
            pltpu.VMEM((2, TOK, 4 * WIDTH), bf16),
            pltpu.SemaphoreType.DMA((4,)),
        ],
        compiler_params=pltpu.CompilerParams(vmem_limit_bytes=16 * MIB),
        name="pack",
    )(ids, *far)


def attend_kernel(in_ref, back_ref, sums_ref, qkg_ref, pd_ref, out_ref, sem):
    scale = 1.0 / math.sqrt(WIDTH)
    count = SEQ * SLOTS
    key, query = iota((count, count), 0), iota((count, count), 1)
    causal, diagonal = key < query, key == query
    spots = [(h, c) for h in range(2) for c in range(0, CL_DEV, 2)]
    for h, c in spots:
        wide = [in_ref[:, x, h, SLOTS * c : SLOTS * (c + 2)].astype(f32) for x in range(4)]
        for s in range(2):
            q32, k32, v32, g32 = [
                w[:, SLOTS * s : SLOTS * (s + 1)].reshape(count, WIDTH) for w in wide
            ]
            q, k, v, g = (x.astype(bf16) for x in (q32, k32, v32, g32))
            for x, y in enumerate((q, k, g)):
                qkg_ref[h, c + s, x] = y
            empty = k32 > LIMIT
            total = jnp.sum(jnp.where(empty, 0.0, k32), axis=0, keepdims=True)
            sums_ref[c + s, h : h + 1] = total * scale
            allowed = (causal & jnp.logical_not(empty)) | diagonal
            score = jnp.where(allowed, dot_nt(k, q) * scale, -1e30)
            dprob = dot_nt(v, g)
            top = jnp.max(score, axis=0, keepdims=True)
            expo = jnp.exp(score - top)
            prob = expo * (1.0 / jnp.sum(expo, axis=0, keepdims=True))
            prob_b = prob.astype(bf16)
            delta = jnp.sum(prob_b.astype(f32) * dprob, axis=0, keepdims=True)
            pd_ref[h, c + s, 0] = prob_b
            pd_ref[h, c + s, 1] = (prob * (dprob - delta) * scale).astype(bf16)
    copies = []
    for h in range(2):
        for x in range(3):
            for c in range(0, CL_DEV, 2):
                halves = []
                for s in range(2):
                    first, second = pd_ref[h, c + s, 0 if x == 2 else 1], qkg_ref[h, c + s, (1, 0, 2)[x]]
                    grad = dot_tn(first, second) if x == 0 else dot(first, second)
                    halves.append(grad.reshape(SEQ, SLOTS, WIDTH))
                tile = jnp.concatenate(halves, axis=1).astype(bf16)
                out_ref[:, x, h, SLOTS * c : SLOTS * (c + 2)] = tile
            copy = pltpu.make_async_copy(out_ref.at[:, x, h], back_ref.at[:, x, h], sem.at[h, x])
            copy.start()
            copies.append(copy)
    for copy in copies:
        copy.wait()


def attend(got):
    return pl.pallas_call(
        attend_kernel,
        in_specs=[WHOLE],
        out_specs=(pl.BlockSpec(memory_space=pltpu.HBM), WHOLE),
        out_shape=(
            pltpu.HBM((SEQ, 3, 2, RUN, WIDTH), bf16),
            jax.ShapeDtypeStruct((CL_DEV, 2, WIDTH), f32),
        ),
        scratch_shapes=[
            pltpu.VMEM((2, CL_DEV, 3, SEQ * SLOTS, WIDTH), bf16),
            pltpu.VMEM((2, CL_DEV, 2, SEQ * SLOTS, SEQ * SLOTS), bf16),
            pltpu.VMEM((SEQ, 3, 2, RUN, WIDTH), bf16),
            pltpu.SemaphoreType.DMA((2, 3)),
        ],
        compiler_params=pltpu.CompilerParams(vmem_limit_bytes=12 * MIB),
        name="attend",
    )(near(got))


def unpack_kernel(half, flat_ref, in_ref, own_ref):
    slot = iota((HALF, ROWS), 1)
    for h in range(2):
        line = flat_ref[h][:, HALF * half : HALF * (half + 1)].astype(f32)
        column = jnp.broadcast_to(line, (8, HALF)).T[:, :1].astype(jnp.int32)
        place = (slot == column).astype(f32).astype(bf16)
        rows = jnp.concatenate([in_ref[:, x, h].reshape(ROWS, WIDTH) for x in range(3)], axis=1)
        own_ref[:, 3 * WIDTH * h : 3 * WIDTH * (h + 1)] = dot(place, rows).astype(bf16)


def unpack(half, flat, home):
    return pl.pallas_call(
        functools.partial(unpack_kernel, half),
        in_specs=[WHOLE, WHOLE],
        out_specs=WHOLE,
        out_shape=pltpu.VMEM((HALF, 6 * WIDTH), bf16),
        compiler_params=pltpu.CompilerParams(vmem_limit_bytes=12 * MIB),
        name="unpack",
    )(flat, near(home))


def merge_kernel(a_ref, b_ref, q_ref, k_ref, v_ref):
    i, j = iota((256, 256), 0), iota((256, 256), 1)
    merge = (i == jnp.where(j < 128, 2 * j, 2 * j - 255)).astype(f32).astype(bf16)
    for s, ref in enumerate((a_ref, b_ref)):
        for b in range(HALF // 128):
            rows = ref[128 * b : 128 * (b + 1), :]
            both = jnp.concatenate([rows[:, : 3 * WIDTH], rows[:, 3 * WIDTH :]], axis=0)
            mixed = dot(merge, both).astype(bf16)
            at = 2 * HALF * s + 256 * b
            q_ref[at : at + 256, :] = mixed[:, :WIDTH]
            k_ref[at : at + 256, :] = mixed[:, WIDTH : 2 * WIDTH]
            v_ref[at : at + 256, :] = mixed[:, 2 * WIDTH :]


def merge(own_a, own_b):
    one = jax.ShapeDtypeStruct((2 * TOK, WIDTH), bf16)
    return pl.pallas_call(
        merge_kernel,
        in_specs=[WHOLE, WHOLE],
        out_specs=(WHOLE,) * 3,
        out_shape=(one, one, one),
        compiler_params=pltpu.CompilerParams(vmem_limit_bytes=6 * MIB),
        cost_estimate=pl.CostEstimate(flops=10**9, bytes_accessed=3 * 10**6, transcendentals=0),
        name="merge",
    )(near(own_a), near(own_b))


def project_kernel(plan, *refs):
    mine_ref, theirs_ref = refs[:2]
    grads, outs = refs[2 : len(refs) - len(plan)], refs[len(refs) - len(plan) :]
    for (at, j), out in zip(plan, outs):
        total = dot(grads[at][...], mine_ref[j]) + dot(grads[at + 1][...], theirs_ref[j])
        out[...] = total.astype(out.dtype)


def project(plan, types, mine, theirs, *grads):
    return pl.pallas_call(
        functools.partial(project_kernel, plan),
        in_specs=[WHOLE] * (2 + len(grads)),
        out_specs=(WHOLE,) * len(plan),
        out_shape=tuple(pltpu.VMEM((HALF, QUARTER), kind) for kind in types),
        compiler_params=pltpu.CompilerParams(vmem_limit_bytes=6 * MIB),
        cost_estimate=pl.CostEstimate(
            flops=len(plan) * 4 * HALF * QUARTER * 6 * WIDTH, bytes_accessed=10**6, transcendentals=0
        ),
        name="project",
    )(*[near(x) for x in (mine, theirs, *grads)])


def finish_kernel(a_ref, b_ref, a_up, a_down, b_up, b_down, out_ref):
    for s, (own, up, down) in enumerate(((a_ref, a_up, a_down), (b_ref, b_up, b_down))):
        total = own[...] + up[...].astype(f32) + down[...].astype(f32)
        out_ref[:, HALF * s : HALF * (s + 1)] = total.T.astype(bf16)


def finish(*parts):
    return pl.pallas_call(
        finish_kernel,
        in_specs=[WHOLE] * 6,
        out_specs=WHOLE,
        out_shape=jax.ShapeDtypeStruct((QUARTER, TOK), bf16),
        compiler_params=pltpu.CompilerParams(vmem_limit_bytes=6 * MIB),
        name="finish",
    )(*[near(x) for x in parts])


def shards(queries, keys, values, out_grad, cluster_ids, query_weight, key_weight, value_weight):
    place = lax.axis_index("head")
    core, z = place % 2, place // 2
    swap = [(i, i ^ 1) for i in range(8)]
    up = [(i, (i + 2) % 8) for i in range(8)]
    down = [(i, (i - 2) % 8) for i in range(8)]

    def blocks(which):
        parts = [w.reshape(4, 2, QUARTER, 2, WIDTH) for w in (query_weight, key_weight, value_weight)]
        parts = [lax.dynamic_index_in_dim(w, which, 1, keepdims=False) for w in parts]
        whole = jnp.transpose(jnp.stack(parts, axis=3), (0, 2, 3, 4, 1)).reshape(4, 6 * WIDTH, QUARTER)
        return jnp.roll(whole, -z, axis=0)

    mine = blocks(core)
    theirs = lax.ppermute(blocks(1 - core), "head", swap)

    ids = jnp.transpose(cluster_ids, (0, 2, 1))
    flat2 = [x.reshape(2 * TOK, WIDTH) for x in (queries, keys, values, out_grad)]
    sent, flat = pack(ids, *flat2)
    got = lax.all_to_all(sent, "seq", split_axis=0, concat_axis=0, tiled=True)
    back, sums = attend(got)
    key_sums = jnp.transpose(sums, (1, 0, 2))
    home = lax.all_to_all(back, "seq", split_axis=0, concat_axis=0, tiled=True)
    home, mine, theirs = lax.optimization_barrier((home, mine, theirs))
    own_a = unpack(0, flat, home)
    other_a = lax.ppermute(own_a, "head", swap)
    own_b = unpack(1, flat, home)
    other_b = lax.ppermute(own_b, "head", swap)

    far_a, down_a = project(((0, 2), (0, 3)), (bf16, bf16), mine, theirs, own_a, other_a)
    far_a = lax.ppermute(far_a, "head", up)
    down_a = lax.ppermute(down_a, "head", down)
    far_b, up_b = project(((0, 2), (0, 1)), (bf16, bf16), mine, theirs, own_b, other_b)
    far_b = lax.ppermute(far_b, "head", down)
    up_b = lax.ppermute(up_b, "head", up)
    next_a, last_b = project(
        ((0, 1), (2, 3)), (f32,) * 2, mine, theirs, own_a, other_a, own_b, other_b
    )
    up_a = lax.ppermute((next_a + far_a.astype(f32)).astype(bf16), "head", up)
    down_b = lax.ppermute((last_b + far_b.astype(f32)).astype(bf16), "head", down)
    own_sum_a, own_sum_b = project(
        ((0, 0), (2, 0)), (f32,) * 2, mine, theirs, own_a, other_a, own_b, other_b
    )
    input_grad = finish(own_sum_a, own_sum_b, up_a, down_a, up_b, down_b)
    grads = [x.reshape(TOK, 2, WIDTH) for x in merge(own_a, own_b)]
    return (*grads, input_grad, key_sums)


def solution(mesh):
    placed = (
        P("seq", "head", None),
        P("seq", "head", None),
        P("seq", "head", None),
        P("seq", "head", None),
        P("head", "seq", None),
        P(None, "head", None),
        P(None, "head", None),
        P(None, "head", None),
    )
    return jax.shard_map(
        shards,
        mesh=mesh,
        in_specs=placed,
        out_specs=(
            P("seq", "head", None),
            P("seq", "head", None),
            P("seq", "head", None),
            P("head", "seq"),
            P("head", "seq", None),
        ),
        check_vma=False,
    )
```

time: 147 us -> 130 us (0.88)
  matrix products: 14.9 us -> 0 us
  waiting for transfers between devices: 17.6 us -> 27.6 us
  local copies, waits for them, and re-layouts: 17.7 us -> 8.77 us
  Pallas kernels: 26.6 us -> 24.1 us
  other arithmetic: 7.35 us -> 4.9 us
    dot_general x12 -> x0, matrix products: 14.9 us -> none  [dot_nt(): lax.dot_general(a, b, (((1,), (1,)), ((), ())), preferred_element_type=f32)]
    unnamed x14 -> x6, local copies, waits for them, and re-layouts: 10.7 us -> 0.7 us
    all_to_all x1, waiting for transfers between devices: 9 us -> 18.2 us  [shards(): home = lax.all_to_all(back, 'seq', split_axis=0, concat_axis=0, tiled=True)]
    pallas_call x3 -> x10, Pallas kernels: 26.6 us -> 24.1 us  [the longest x2 7.66 us: unpack(): pl.pallas_call(functools.partial(unpack_kernel, half), in_specs=[WHOLE, W...]
    dynamic_slice x2 -> x8, local copies, waits for them, and re-layouts: 6.92 us -> 8.07 us  [blocks(): lax.dynamic_index_in_dim(w, which, 1, keepdims=False)]
    ppermute x8 -> x9, starting transfers between devices: 11 us -> 11.9 us  [the longest x1 4.1 us: shards(): far_b = lax.ppermute(far_b, 'head', down)]
    ppermute x8 -> x9, waiting for transfers between devices: 8.6 us -> 9.41 us  [the longest x1 4.36 us: shards(): up_a = lax.ppermute((next_a + far_a.astype(f32)).astype(bf16), 'head', up)]
    another operation x3 -> x2, other arithmetic: 3 us -> 2.43 us  [blocks(): jnp.stack(parts, axis=3)]
  transfers between devices with their start and end apart: 9 -> 10, of which waited for: 4 -> 5; matrix products, arithmetic and copies ran while one was open for 24% -> 10% of each run, Pallas kernels for 6% -> 7%
where the time goes in v2:
time: 130 us; the launch traced here: 129 us
  blocking collectives  46.4 us (36%)
  waiting for transfers between devices  27.6 us (21%)
  Pallas kernels  24.1 us (19%)
  starting transfers between devices  16.5 us (13%)
  local copies, waits for them, and re-layouts  8.77 us (7%)
  other arithmetic  4.9 us (4%)
    all_to_all x1, blocking collectives, shards(): got = lax.all_to_all(sent, 'seq', split_axis=0, concat_axis=0, tiled=True)  46.4 us
    all_to_all x1, waiting for transfers between devices, shards(): home = lax.all_to_all(back, 'seq', split_axis=0, concat_axis=0, tiled=True)  18.2 us
    dynamic_slice x8, local copies, waits for them, and re-layouts, blocks(): lax.dynamic_index_in_dim(w, which, 1, keepdims=False)  8.07 us
    pallas_call x2, Pallas kernels, unpack(): pl.pallas_call(functools.partial(unpack_kernel, half), in_specs=[WHOLE, W...  7.66 us
    pallas_call x1, Pallas kernels, pack(): pl.pallas_call(pack_kernel, in_specs=[WHOLE] + [pl.BlockSpec(memory_space...  5.53 us
    all_to_all x1, starting transfers between devices, shards(): home = lax.all_to_all(back, 'seq', split_axis=0, concat_axis=0, tiled=True)  4.59 us
    ppermute x1, waiting for transfers between devices, shards(): up_a = lax.ppermute((next_a + far_a.astype(f32)).astype(bf16), 'head', up)  4.36 us
    pallas_call x1, Pallas kernels, attend(): pl.pallas_call(attend_kernel, in_specs=[WHOLE], out_specs=(pl.BlockSpec(m...  4.13 us
  transfers between devices with their start and end apart: 10, of which 5 were waited for; matrix products, arithmetic and copies ran while one was open for 10% of the time, Pallas kernels for 7%

profile of v2, /device:TPU:0, one launch (start us, length us, event | category | flops | bytes accessed | tf_op | source)
XLA Modules:
  0.0 129.2 jit_solution(579224463571877090)
XLA Ops:
  0.6 0.7 copy-done
  1.3 5.5 %pack.1 = (bf16[16,4,2,96,128]{4,3,2,1,0:T(8,128)(2,1)S(1)}, s32[2,1,1024]{2,1,0:T(1,128)S(1)}) custom-call(s32[2,1,1024]{2,1,0:T(1,128)S(1)} %bitcast.24, bf16[2048,128]{1,0:T(8,128)(2,1)} %bitcast.36, bf16[2048,128]{1,0:T(8,128)(2,1)} %bitcast.37, bf16[2048,128]{1,0:T(8,128)(2,1)} %bitcast.38, bf16[2048,128]{1,0:T(8,128)(2,1)} %bitcast.39), custom_call_target="tpu_custom_call" | custom-call | tf_op jit(solution)/shard_map/pack/pallas_call | solution.py:107
  6.9 46.4 %all_to_all.10.in_ref = bf16[16,4,2,96,128]{4,3,2,1,0:T(8,128)(2,1)S(1)} all-to-all(bf16[16,4,2,96,128]{4,3,2,1,0:T(8,128)(2,1)S(1)} %get-tuple-element.25), channel_id=1, replica_groups=mesh['head'=8,'seq'=16] {'seq'}, dimensions={0} | all-to-all | bytes 6291456 | tf_op jit(solution)/shard_map/all_to_all | solution.py:297
  53.3 4.1 %attend.1 = (bf16[16,3,2,96,128]{4,3,2,1,0:T(8,128)(2,1)}, f32[12,2,128]{2,1,0:T(2,128)}) custom-call(bf16[16,4,2,96,128]{4,3,2,1,0:T(8,128)(2,1)S(1)} %all_to_all.10.in_ref), custom_call_target="tpu_custom_call" | custom-call | tf_op jit(solution)/shard_map/attend/pallas_call | solution.py:172
  57.4 4.6 %all-to-all-start.1 = ((bf16[16,3,2,96,128]{4,3,2,1,0:T(8,128)(2,1)}), bf16[16,3,2,96,128]{4,3,2,1,0:T(8,128)(2,1)}, u32[]{:S(2)}, u32[]{:S(2)}) async-start(bf16[16,3,2,96,128]{4,3,2,1,0:T(8,128)(2,1)} %get-tuple-element.26), calls=%async_computation.1 | async-start | bytes 4718592 | tf_op jit(solution)/shard_map/all_to_all | solution.py:300
  62.1 0.7 constant_dynamic-slice_fusion.2
  62.8 0.4 copy.16
  63.2 3.1 %constant_dynamic-slice_fusion = (bf16[4,1,256,2,128]{4,3,2,1,0:T(2,128)(2,1)S(1)}, bf16[4,1,256,2,128]{4,3,2,1,0:T(2,128)(2,1)S(1)}, bf16[4,1,256,2,128]{4,3,2,...) fusion(bf16[4,2,256,2,128]{4,3,2,1,0:T(2,128)(2,1)} %bitcast.33, s32[]{:T(128)S(6)} %select_n.34, s32[]{:T(128)S(6)} %select_n.32, ...), kind=kLoop, calls=%fused_computation.10 | loop fusion | bytes 4194312 | tf_op jit(solution)/shard_map/jit(dynamic_index_in_dim)/dynamic_slice | solution.py:287
  66.3 1.1 copy.18
  67.7 1.2 pad_maximum_fusion.1
  68.9 1.8 %fusion = bf16[4,768,256]{2,1,0:T(8,128)(2,1)} fusion(s32[]{:T(128)S(6)} %select_n.38, bf16[4,768,256]{2,1,0:T(8,128)(2,1)S(1)} %bitcast.26), kind=kLoop, calls=%fused_computation.4 | loop fusion | flops 786432 | bytes 3145732 | tf_op jit(solution)/shard_map/jit(_roll_dynamic)/concatenate | solution.py:289
  70.7 1.1 copy.13
  71.8 1.1 copy.15
  73.2 1.2 pad_maximum_fusion
  74.4 0.6 fusion.1.refs_0_
  75.0 18.2 %all-to-all-done.1.in_ref = bf16[16,3,2,96,128]{4,3,2,1,0:T(8,128)(2,1)} async-done(((bf16[16,3,2,96,128]{4,3,2,1,0:T(8,128)(2,1)}), bf16[16,3,2,96,128]{4,3,2,1,0:T(8,128)(2,1)}, u32[]{:S(2)}, u32[]{:S(2)}) %all-to-all-start.1) | async-done | bytes 2359328 | tf_op jit(solution)/shard_map/all_to_all | solution.py:300
  93.2 3.8 %unpack.3.b_ref.refs_4_.refs_2_ = bf16[512,768]{1,0:T(8,128)(2,1)S(1)} custom-call(s32[2,1,1024]{2,1,0:T(1,128)S(1)} %get-tuple-element.24.flat_ref, bf16[16,3,2,96,128]{4,3,2,1,0:T(8,128)(2,1)} %all-to-all-done.1.in_ref), custom_call_target="tpu_custom_call" | custom-call | tf_op jit(solution)/shard_map/unpack/pallas_call | solution.py:202
  97.2 3.8 %unpack.2.a_ref.refs_2_ = bf16[512,768]{1,0:T(8,128)(2,1)S(1)} custom-call(s32[2,1,1024]{2,1,0:T(1,128)S(1)} %get-tuple-element.24.flat_ref, bf16[16,3,2,96,128]{4,3,2,1,0:T(8,128)(2,1)} %all-to-all-done.1.in_ref), custom_call_target="tpu_custom_call" | custom-call | tf_op jit(solution)/shard_map/unpack/pallas_call | solution.py:202
  101.0 0.6 collective-permute-start.1
  101.6 1.0 project.7
  102.6 4.1 %collective-permute-start.7 = (bf16[512,256]{1,0:T(8,128)(2,1)S(1)}, bf16[512,256]{1,0:T(8,128)(2,1)S(1)}, u32[]{:S(2)}, u32[]{:S(2)}) collective-permute-start(bf16[512,256]{1,0:T(8,128)(2,1)S(1)} %get-tuple-element.40), channel_id=1, source_target_pairs={{0,96},{16,112},{32,0},{48,16},{64,32},{80,48},{96,64},{112,80},{1... | collective-permute-start | bytes 786440 | tf_op jit(solution)/shard_map/ppermute | solution.py:311
  106.7 1.0 project.6
  107.8 3.2 %collective-permute-start.5 = (bf16[512,256]{1,0:T(8,128)(2,1)S(1)}, bf16[512,256]{1,0:T(8,128)(2,1)S(1)}, u32[]{:S(2)}, u32[]{:S(2)}) collective-permute-start(bf16[512,256]{1,0:T(8,128)(2,1)S(1)} %get-tuple-element.37), channel_id=1, source_target_pairs={{0,96},{16,112},{32,0},{48,16},{64,32},{80,48},{96,64},{112,80},{1... | collective-permute-start | bytes 786440 | tf_op jit(solution)/shard_map/ppermute | solution.py:309
  111.0 1.0 project.5
  112.0 1.4 %collective-permute-done.7 = bf16[512,256]{1,0:T(8,128)(2,1)S(1)} collective-permute-done((bf16[512,256]{1,0:T(8,128)(2,1)S(1)}, bf16[512,256]{1,0:T(8,128)(2,1)S(1)}, u32[]{:S(2)}, u32[]{:S(2)}) %collective-permute-start.7) | collective-permute-done | bytes 262176 | tf_op jit(solution)/shard_map/ppermute | solution.py:311
  113.4 3.8 %collective-permute-start.8 = (bf16[512,256]{1,0:T(8,128)(2,1)S(1)}, bf16[512,256]{1,0:T(8,128)(2,1)S(1)}, u32[]{:S(2)}, u32[]{:S(2)}) collective-permute-start(bf16[512,256]{1,0:T(8,128)(2,1)S(1)} %add_convert_fusion), channel_id=1, source_target_pairs={{0,96},{16,112},{32,0},{48,16},{64,32},{80,48},{96,64},{112,80},{1... | collective-permute-start | bytes 786440 | tf_op jit(solution)/shard_map/ppermute | solution.py:317
  117.2 1.0 collective-permute-done.3
  118.3 1.8 %merge.1 = (bf16[2048,128]{1,0:T(8,128)(2,1)}, bf16[2048,128]{1,0:T(8,128)(2,1)}, bf16[2048,128]{1,0:T(8,128)(2,1)}) custom-call(bf16[512,768]{1,0:T(8,128)(2,1)S(1)} %unpack.2.a_ref.refs_2_, bf16[512,768]{1,0:T(8,128)(2,1)S(1)} %unpack.3.b_ref.refs_4_.refs_2_), custom_call_target="tpu_custom_call" | custom-call | flops 1000000000 | bytes 3000000 | tf_op jit(solution)/shard_map/merge/pallas_call | solution.py:228
  120.1 1.0 project.4
  121.1 2.7 %collective-permute-done.6.b_up = bf16[512,256]{1,0:T(8,128)(2,1)S(1)} collective-permute-done((bf16[512,256]{1,0:T(8,128)(2,1)S(1)}, bf16[512,256]{1,0:T(8,128)(2,1)S(1)}, u32[]{:S(2)}, u32[]{:S(2)}) %collective-permute-start.6) | collective-permute-done | bytes 262176 | tf_op jit(solution)/shard_map/ppermute | solution.py:312
  123.8 4.4 %collective-permute-done.4.a_up = bf16[512,256]{1,0:T(8,128)(2,1)S(1)} collective-permute-done((bf16[512,256]{1,0:T(8,128)(2,1)S(1)}, bf16[512,256]{1,0:T(8,128)(2,1)S(1)}, u32[]{:S(2)}, u32[]{:S(2)}) %collective-permute-start.4) | collective-permute-done | bytes 262176 | tf_op jit(solution)/shard_map/ppermute | solution.py:316
  128.1 1.1 finish.1
  (19 shorter events, 1.1 us)
Async XLA Ops:
  0.6 0.7 copy-start
  57.4 4.7 %copy-start.2 = (bf16[2048,2,128]{2,1,0:T(2,128)(2,1)S(1)}, bf16[2048,2,128]{2,1,0:T(2,128)(2,1)}, u32[]{:S(2)}) copy-start(bf16[2048,2,128]{2,1,0:T(2,128)(2,1)} %param.15) | copy-start | bytes 3145732
  57.4 35.8 %all-to-all-start.1 = ((bf16[16,3,2,96,128]{4,3,2,1,0:T(8,128)(2,1)}), bf16[16,3,2,96,128]{4,3,2,1,0:T(8,128)(2,1)}, u32[]{:S(2)}, u32[]{:S(2)}) async-start(bf16[16,3,2,96,128]{4,3,2,1,0:T(8,128)(2,1)} %get-tuple-element.26), calls=%async_computation.1 | async-start | bytes 4718592 | tf_op jit(solution)/shard_map/all_to_all | solution.py:300
  70.7 4.3 %collective-permute-start = (bf16[4,768,256]{2,1,0:T(8,128)(2,1)}, bf16[4,768,256]{2,1,0:T(8,128)(2,1)S(1)}, u32[]{:S(2)}, u32[]{:S(2)}) collective-permute-start(bf16[4,768,256]{2,1,0:T(8,128)(2,1)} %fusion), channel_id=1, source_target_pairs={{0,16},{16,0},{32,48},{48,32},{64,80},{80,64},{96,112},{112,96},{1... | collective-permute-start | bytes 4718600 | tf_op jit(solution)/shard_map/ppermute | solution.py:292
  71.8 1.4 %copy-start.1 = (bf16[4,1,256,2,128]{2,4,3,0,1:T(8,128)(2,1)S(1)}, bf16[4,1,256,2,128]{2,4,3,0,1:T(8,128)(2,1)}, u32[]{:S(2)}) copy-start(bf16[4,1,256,2,128]{2,4,3,0,1:T(8,128)(2,1)} %copy.13) | copy-start | bytes 1572868
  97.1 4.5 %collective-permute-start.2 = (bf16[512,768]{1,0:T(8,128)(2,1)S(1)}, bf16[512,768]{1,0:T(8,128)(2,1)S(1)}, u32[]{:S(2)}, u32[]{:S(2)}) collective-permute-start(bf16[512,768]{1,0:T(8,128)(2,1)S(1)} %unpack.3.b_ref.refs_4_.refs_2_), channel_id=1, source_target_pairs={{0,16},{16,0},{32,48},{48,32},{64,80},{80,64},{96,112},{112,96},{1... | collective-permute-start | bytes 2359304 | tf_op jit(solution)/shard_map/ppermute | solution.py:305
  101.0 5.7 %collective-permute-start.1 = (bf16[512,768]{1,0:T(8,128)(2,1)S(1)}, bf16[512,768]{1,0:T(8,128)(2,1)S(1)}, u32[]{:S(2)}, u32[]{:S(2)}) collective-permute-start(bf16[512,768]{1,0:T(8,128)(2,1)S(1)} %unpack.2.a_ref.refs_2_), channel_id=1, source_target_pairs={{0,16},{16,0},{32,48},{48,32},{64,80},{80,64},{96,112},{112,96},{1... | collective-permute-start | bytes 2359304 | tf_op jit(solution)/shard_map/ppermute | solution.py:303
  102.6 10.8 %collective-permute-start.7 = (bf16[512,256]{1,0:T(8,128)(2,1)S(1)}, bf16[512,256]{1,0:T(8,128)(2,1)S(1)}, u32[]{:S(2)}, u32[]{:S(2)}) collective-permute-start(bf16[512,256]{1,0:T(8,128)(2,1)S(1)} %get-tuple-element.40), channel_id=1, source_target_pairs={{0,96},{16,112},{32,0},{48,16},{64,32},{80,48},{96,64},{112,80},{1... | collective-permute-start | bytes 786440 | tf_op jit(solution)/shard_map/ppermute | solution.py:311
  107.7 10.5 %collective-permute-start.3 = (bf16[512,256]{1,0:T(8,128)(2,1)S(1)}, bf16[512,256]{1,0:T(8,128)(2,1)S(1)}, u32[]{:S(2)}, u32[]{:S(2)}) collective-permute-start(bf16[512,256]{1,0:T(8,128)(2,1)S(1)} %get-tuple-element.36), channel_id=1, source_target_pairs={{0,32},{16,48},{32,64},{48,80},{64,96},{80,112},{96,0},{112,16},{1... | collective-permute-start | bytes 786440 | tf_op jit(solution)/shard_map/ppermute | solution.py:308
  107.8 13.4 %collective-permute-start.5 = (bf16[512,256]{1,0:T(8,128)(2,1)S(1)}, bf16[512,256]{1,0:T(8,128)(2,1)S(1)}, u32[]{:S(2)}, u32[]{:S(2)}) collective-permute-start(bf16[512,256]{1,0:T(8,128)(2,1)S(1)} %get-tuple-element.37), channel_id=1, source_target_pairs={{0,96},{16,112},{32,0},{48,16},{64,32},{80,48},{96,64},{112,80},{1... | collective-permute-start | bytes 786440 | tf_op jit(solution)/shard_map/ppermute | solution.py:309
  111.0 12.8 %collective-permute-start.6 = (bf16[512,256]{1,0:T(8,128)(2,1)S(1)}, bf16[512,256]{1,0:T(8,128)(2,1)S(1)}, u32[]{:S(2)}, u32[]{:S(2)}) collective-permute-start(bf16[512,256]{1,0:T(8,128)(2,1)S(1)} %get-tuple-element.38), channel_id=1, source_target_pairs={{0,32},{16,48},{32,64},{48,80},{64,96},{80,112},{96,0},{112,16},{1... | collective-permute-start | bytes 786440 | tf_op jit(solution)/shard_map/ppermute | solution.py:312
  113.4 10.3 %collective-permute-start.8 = (bf16[512,256]{1,0:T(8,128)(2,1)S(1)}, bf16[512,256]{1,0:T(8,128)(2,1)S(1)}, u32[]{:S(2)}, u32[]{:S(2)}) collective-permute-start(bf16[512,256]{1,0:T(8,128)(2,1)S(1)} %add_convert_fusion), channel_id=1, source_target_pairs={{0,96},{16,112},{32,0},{48,16},{64,32},{80,48},{96,64},{112,80},{1... | collective-permute-start | bytes 786440 | tf_op jit(solution)/shard_map/ppermute | solution.py:317
  118.2 9.9 %collective-permute-start.4 = (bf16[512,256]{1,0:T(8,128)(2,1)S(1)}, bf16[512,256]{1,0:T(8,128)(2,1)S(1)}, u32[]{:S(2)}, u32[]{:S(2)}) collective-permute-start(bf16[512,256]{1,0:T(8,128)(2,1)S(1)} %add_convert_fusion.1), channel_id=1, source_target_pairs={{0,32},{16,48},{32,64},{48,80},{64,96},{80,112},{96,0},{112,16},{1... | collective-permute-start | bytes 786440 | tf_op jit(solution)/shard_map/ppermute | solution.py:316

commit v3 on v2

--- a/solution.py
+++ b/solution.py
@@ -188,25 +188,63 @@
     )(near(got))
 
 
-def unpack_kernel(half, flat_ref, in_ref, own_ref):
+def gather(h, rows_ref, own_ref, place):
+    rows = jnp.concatenate([rows_ref[h, x].reshape(ROWS, WIDTH) for x in range(3)], axis=1)
+    own_ref[:, 3 * WIDTH * h : 3 * WIDTH * (h + 1)] = dot(place, rows).astype(bf16)
+
+
+def places(half, h, flat_ref):
     slot = iota((HALF, ROWS), 1)
-    for h in range(2):
-        line = flat_ref[h][:, HALF * half : HALF * (half + 1)].astype(f32)
-        column = jnp.broadcast_to(line, (8, HALF)).T[:, :1].astype(jnp.int32)
-        place = (slot == column).astype(f32).astype(bf16)
-        rows = jnp.concatenate([in_ref[:, x, h].reshape(ROWS, WIDTH) for x in range(3)], axis=1)
-        own_ref[:, 3 * WIDTH * h : 3 * WIDTH * (h + 1)] = dot(place, rows).astype(bf16)
-
-
-def unpack(half, flat, home):
-    return pl.pallas_call(
-        functools.partial(unpack_kernel, half),
+    line = flat_ref[h][:, HALF * half : HALF * (half + 1)].astype(f32)
+    column = jnp.broadcast_to(line, (8, HALF)).T[:, :1].astype(jnp.int32)
+    column = jnp.broadcast_to(column, slot.shape).astype(jnp.int16)
+    return jnp.where(slot.astype(jnp.int16) == column, bf16(1), bf16(0))
+
+
+def unpack_first_kernel(flat_ref, home_ref, own_ref, rows_ref, place_ref, sem):
+    copies = []
+    for h in range(2):
+        for x in range(3):
+            copy = pltpu.make_async_copy(home_ref.at[:, x, h], rows_ref.at[h, x], sem.at[h, x])
+            copy.start()
+            copies.append(copy)
+    for h in range(2):
+        place_ref[h] = places(1, h, flat_ref)
+    for h in range(2):
+        for copy in copies[3 * h : 3 * h + 3]:
+            copy.wait()
+        gather(h, rows_ref, own_ref, place_ref[h])
+
+
+def unpack_first(flat, home):
+    return pl.pallas_call(
+        unpack_first_kernel,
+        in_specs=[WHOLE, pl.BlockSpec(memory_space=pltpu.HBM)],
+        out_specs=(WHOLE, WHOLE),
+        out_shape=(
+            pltpu.VMEM((HALF, 6 * WIDTH), bf16),
+            pltpu.VMEM((2, 3, SEQ, RUN, WIDTH), bf16),
+        ),
+        scratch_shapes=[pltpu.VMEM((2, HALF, ROWS), bf16), pltpu.SemaphoreType.DMA((2, 3))],
+        compiler_params=pltpu.CompilerParams(vmem_limit_bytes=16 * MIB),
+        name="unpack_first",
+    )(flat, pltpu.with_memory_space_constraint(home, pltpu.HBM))
+
+
+def unpack_last_kernel(flat_ref, rows_ref, own_ref):
+    for h in range(2):
+        gather(h, rows_ref, own_ref, places(0, h, flat_ref))
+
+
+def unpack_last(flat, rows):
+    return pl.pallas_call(
+        unpack_last_kernel,
         in_specs=[WHOLE, WHOLE],
         out_specs=WHOLE,
         out_shape=pltpu.VMEM((HALF, 6 * WIDTH), bf16),
         compiler_params=pltpu.CompilerParams(vmem_limit_bytes=12 * MIB),
-        name="unpack",
-    )(flat, near(home))
+        name="unpack_last",
+    )(flat, near(rows))
 
 
 def merge_kernel(a_ref, b_ref, q_ref, k_ref, v_ref):
@@ -298,11 +336,11 @@
     back, sums = attend(got)
     key_sums = jnp.transpose(sums, (1, 0, 2))
     home = lax.all_to_all(back, "seq", split_axis=0, concat_axis=0, tiled=True)
-    home, mine, theirs = lax.optimization_barrier((home, mine, theirs))
-    own_a = unpack(0, flat, home)
+    flat, mine, theirs = lax.optimization_barrier((flat, mine, theirs))
+    own_b, rows = unpack_first(flat, home)
+    other_b = lax.ppermute(own_b, "head", swap)
+    own_a = unpack_last(flat, rows)
     other_a = lax.ppermute(own_a, "head", swap)
-    own_b = unpack(1, flat, home)
-    other_b = lax.ppermute(own_b, "head", swap)
 
     far_a, down_a = project(((0, 2), (0, 3)), (bf16, bf16), mine, theirs, own_a, other_a)
     far_a = lax.ppermute(far_a, "head", up)

time: 130 us -> 127 us (0.977)
  Pallas kernels: 24.1 us -> 21.7 us
    pallas_call x2, Pallas kernels: 7.66 us -> 5.3 us  [the longest x1 3.25 us: unpack_first(): pl.pallas_call(unpack_first_kernel, in_specs=[WHOLE, pl.BlockSpec(memory_...]
  transfers between devices with their start and end apart: 10 -> 10, of which waited for: 5 -> 5; matrix products, arithmetic and copies ran while one was open for 10% -> 10% of each run, Pallas kernels for 7% -> 6%
where the time goes in v3:
time: 127 us
  blocking collectives  46.4 us (37%)
  waiting for transfers between devices  27.7 us (22%)
  Pallas kernels  21.7 us (17%)
  starting transfers between devices  16.5 us (13%)
  local copies, waits for them, and re-layouts  8.77 us (7%)
  other arithmetic  4.88 us (4%)
    all_to_all x1, blocking collectives, shards(): got = lax.all_to_all(sent, 'seq', split_axis=0, concat_axis=0, tiled=True)  46.4 us
    all_to_all x1, waiting for transfers between devices, shards(): home = lax.all_to_all(back, 'seq', split_axis=0, concat_axis=0, tiled=True)  18.3 us
    dynamic_slice x8, local copies, waits for them, and re-layouts, blocks(): lax.dynamic_index_in_dim(w, which, 1, keepdims=False)  8.07 us
    pallas_call x1, Pallas kernels, pack(): pl.pallas_call(pack_kernel, in_specs=[WHOLE] + [pl.BlockSpec(memory_space...  5.53 us
    all_to_all x1, starting transfers between devices, shards(): home = lax.all_to_all(back, 'seq', split_axis=0, concat_axis=0, tiled=True)  4.58 us
    ppermute x1, waiting for transfers between devices, shards(): up_a = lax.ppermute((next_a + far_a.astype(f32)).astype(bf16), 'head', up)  4.36 us
    ppermute x1, starting transfers between devices, shards(): far_b = lax.ppermute(far_b, 'head', down)  4.12 us
    pallas_call x1, Pallas kernels, attend(): pl.pallas_call(attend_kernel, in_specs=[WHOLE], out_specs=(pl.BlockSpec(m...  4.04 us
  transfers between devices with their start and end apart: 10, of which 5 were waited for; matrix products, arithmetic and copies ran while one was open for 10% of the time, Pallas kernels for 6%

profile of v3, /device:TPU:0, one launch (start us, length us, event | category | flops | bytes accessed | tf_op | source)
XLA Modules:
  0.0 126.8 jit_solution(1521198362679058466)
XLA Ops:
  0.6 0.7 copy-done
  1.3 5.5 %pack.1 = (bf16[16,4,2,96,128]{4,3,2,1,0:T(8,128)(2,1)S(1)}, s32[2,1,1024]{2,1,0:T(1,128)S(1)}) custom-call(s32[2,1,1024]{2,1,0:T(1,128)S(1)} %bitcast.24, bf16[2048,128]{1,0:T(8,128)(2,1)} %bitcast.36, bf16[2048,128]{1,0:T(8,128)(2,1)} %bitcast.37, bf16[2048,128]{1,0:T(8,128)(2,1)} %bitcast.38, bf16[2048,128]{1,0:T(8,128)(2,1)} %bitcast.39), custom_call_target="tpu_custom_call" | custom-call | tf_op jit(solution)/shard_map/pack/pallas_call | solution.py:107
  6.9 46.4 %all_to_all.10.in_ref = bf16[16,4,2,96,128]{4,3,2,1,0:T(8,128)(2,1)S(1)} all-to-all(bf16[16,4,2,96,128]{4,3,2,1,0:T(8,128)(2,1)S(1)} %get-tuple-element.28), channel_id=1, replica_groups=mesh['head'=8,'seq'=16] {'seq'}, dimensions={0} | all-to-all | bytes 6291456 | tf_op jit(solution)/shard_map/all_to_all | solution.py:335
  53.3 4.0 %attend.1 = (bf16[16,3,2,96,128]{4,3,2,1,0:T(8,128)(2,1)}, f32[12,2,128]{2,1,0:T(2,128)}) custom-call(bf16[16,4,2,96,128]{4,3,2,1,0:T(8,128)(2,1)S(1)} %all_to_all.10.in_ref), custom_call_target="tpu_custom_call" | custom-call | tf_op jit(solution)/shard_map/attend/pallas_call | solution.py:172
  57.3 4.6 %all-to-all-start.1 = ((bf16[16,3,2,96,128]{4,3,2,1,0:T(8,128)(2,1)}), bf16[16,3,2,96,128]{4,3,2,1,0:T(8,128)(2,1)}, u32[]{:S(2)}, u32[]{:S(2)}) async-start(bf16[16,3,2,96,128]{4,3,2,1,0:T(8,128)(2,1)} %get-tuple-element.29), calls=%async_computation.1 | async-start | bytes 4718592 | tf_op jit(solution)/shard_map/all_to_all | solution.py:338
  62.0 0.7 constant_dynamic-slice_fusion.2
  62.7 0.4 copy.16
  63.1 3.1 %constant_dynamic-slice_fusion = (bf16[4,1,256,2,128]{4,3,2,1,0:T(2,128)(2,1)S(1)}, bf16[4,1,256,2,128]{4,3,2,1,0:T(2,128)(2,1)S(1)}, bf16[4,1,256,2,128]{4,3,2,...) fusion(bf16[4,2,256,2,128]{4,3,2,1,0:T(2,128)(2,1)} %bitcast.33, s32[]{:T(128)S(6)} %select_n.34, s32[]{:T(128)S(6)} %select_n.32, ...), kind=kLoop, calls=%fused_computation.10 | loop fusion | bytes 4194312 | tf_op jit(solution)/shard_map/jit(dynamic_index_in_dim)/dynamic_slice | solution.py:325
  66.2 1.1 copy.18
  67.6 1.2 pad_maximum_fusion.1
  68.8 1.8 %fusion = bf16[4,768,256]{2,1,0:T(8,128)(2,1)} fusion(s32[]{:T(128)S(6)} %select_n.38, bf16[4,768,256]{2,1,0:T(8,128)(2,1)S(1)} %bitcast.26), kind=kLoop, calls=%fused_computation.4 | loop fusion | flops 786432 | bytes 3145732 | tf_op jit(solution)/shard_map/jit(_roll_dynamic)/concatenate | solution.py:327
  70.6 1.1 copy.13
  71.6 1.1 copy.15
  73.1 1.2 pad_maximum_fusion
  74.3 0.6 fusion.1.refs_0_
  74.9 18.3 %all-to-all-done.1.home_ref = bf16[16,3,2,96,128]{4,3,2,1,0:T(8,128)(2,1)} async-done(((bf16[16,3,2,96,128]{4,3,2,1,0:T(8,128)(2,1)}), bf16[16,3,2,96,128]{4,3,2,1,0:T(8,128)(2,1)}, u32[]{:S(2)}, u32[]{:S(2)}) %all-to-all-start.1) | async-done | bytes 2359328 | tf_op jit(solution)/shard_map/all_to_all | solution.py:338
  93.2 3.2 %unpack_first.1 = (bf16[512,768]{1,0:T(8,128)(2,1)S(1)}, bf16[2,3,16,96,128]{4,3,2,1,0:T(8,128)(2,1)S(1)}) custom-call(s32[2,1,1024]{2,1,0:T(1,128)S(1)} %get-tuple-element.27.flat_ref, bf16[16,3,2,96,128]{4,3,2,1,0:T(8,128)(2,1)} %all-to-all-done.1.home_ref), custom_call_target="tpu_custom_call" | custom-call | tf_op jit(solution)/shard_map/unpack_first/pallas_call | solution.py:220
  96.5 2.1 %unpack_last.1.a_ref.refs_2_ = bf16[512,768]{1,0:T(8,128)(2,1)S(1)} custom-call(s32[2,1,1024]{2,1,0:T(1,128)S(1)} %get-tuple-element.27.flat_ref, bf16[2,3,16,96,128]{4,3,2,1,0:T(8,128)(2,1)S(1)} %get-tuple-element.30.rows_ref), custom_call_target="tpu_custom_call" | custom-call | tf_op jit(solution)/shard_map/unpack_last/pallas_call | solution.py:240
  98.6 0.6 collective-permute-start.1
  99.1 1.0 project.7
  100.1 4.1 %collective-permute-start.7 = (bf16[512,256]{1,0:T(8,128)(2,1)S(1)}, bf16[512,256]{1,0:T(8,128)(2,1)S(1)}, u32[]{:S(2)}, u32[]{:S(2)}) collective-permute-start(bf16[512,256]{1,0:T(8,128)(2,1)S(1)} %get-tuple-element.44), channel_id=1, source_target_pairs={{0,96},{16,112},{32,0},{48,16},{64,32},{80,48},{96,64},{112,80},{1... | collective-permute-start | bytes 786440 | tf_op jit(solution)/shard_map/ppermute | solution.py:349
  104.2 1.0 project.6
  105.3 3.2 %collective-permute-start.5 = (bf16[512,256]{1,0:T(8,128)(2,1)S(1)}, bf16[512,256]{1,0:T(8,128)(2,1)S(1)}, u32[]{:S(2)}, u32[]{:S(2)}) collective-permute-start(bf16[512,256]{1,0:T(8,128)(2,1)S(1)} %get-tuple-element.41), channel_id=1, source_target_pairs={{0,96},{16,112},{32,0},{48,16},{64,32},{80,48},{96,64},{112,80},{1... | collective-permute-start | bytes 786440 | tf_op jit(solution)/shard_map/ppermute | solution.py:347
  108.5 1.0 project.5
  109.5 1.4 %collective-permute-done.7 = bf16[512,256]{1,0:T(8,128)(2,1)S(1)} collective-permute-done((bf16[512,256]{1,0:T(8,128)(2,1)S(1)}, bf16[512,256]{1,0:T(8,128)(2,1)S(1)}, u32[]{:S(2)}, u32[]{:S(2)}) %collective-permute-start.7) | collective-permute-done | bytes 262176 | tf_op jit(solution)/shard_map/ppermute | solution.py:349
  111.0 3.8 %collective-permute-start.8 = (bf16[512,256]{1,0:T(8,128)(2,1)S(1)}, bf16[512,256]{1,0:T(8,128)(2,1)S(1)}, u32[]{:S(2)}, u32[]{:S(2)}) collective-permute-start(bf16[512,256]{1,0:T(8,128)(2,1)S(1)} %add_convert_fusion), channel_id=1, source_target_pairs={{0,96},{16,112},{32,0},{48,16},{64,32},{80,48},{96,64},{112,80},{1... | collective-permute-start | bytes 786440 | tf_op jit(solution)/shard_map/ppermute | solution.py:355
  114.7 1.0 collective-permute-done.3
  115.9 1.8 %merge.1 = (bf16[2048,128]{1,0:T(8,128)(2,1)}, bf16[2048,128]{1,0:T(8,128)(2,1)}, bf16[2048,128]{1,0:T(8,128)(2,1)}) custom-call(bf16[512,768]{1,0:T(8,128)(2,1)S(1)} %unpack_last.1.a_ref.refs_2_, bf16[512,768]{1,0:T(8,128)(2,1)S(1)} %get-tuple-element.31.b_ref.refs_4_.refs_2_), custom_call_target="tpu_custom_call" | custom-call | flops 1000000000 | bytes 3000000 | tf_op jit(solution)/shard_map/merge/pallas_call | solution.py:266
  117.7 1.0 project.4
  118.7 2.7 %collective-permute-done.6.b_up = bf16[512,256]{1,0:T(8,128)(2,1)S(1)} collective-permute-done((bf16[512,256]{1,0:T(8,128)(2,1)S(1)}, bf16[512,256]{1,0:T(8,128)(2,1)S(1)}, u32[]{:S(2)}, u32[]{:S(2)}) %collective-permute-start.6) | collective-permute-done | bytes 262176 | tf_op jit(solution)/shard_map/ppermute | solution.py:350
  121.3 4.4 %collective-permute-done.4.a_up = bf16[512,256]{1,0:T(8,128)(2,1)S(1)} collective-permute-done((bf16[512,256]{1,0:T(8,128)(2,1)S(1)}, bf16[512,256]{1,0:T(8,128)(2,1)S(1)}, u32[]{:S(2)}, u32[]{:S(2)}) %collective-permute-start.4) | collective-permute-done | bytes 262176 | tf_op jit(solution)/shard_map/ppermute | solution.py:354
  125.7 1.1 finish.1
  (19 shorter events, 1.1 us)
Async XLA Ops:
  0.6 0.7 copy-start
  57.3 4.7 %copy-start.2 = (bf16[2048,2,128]{2,1,0:T(2,128)(2,1)S(1)}, bf16[2048,2,128]{2,1,0:T(2,128)(2,1)}, u32[]{:S(2)}) copy-start(bf16[2048,2,128]{2,1,0:T(2,128)(2,1)} %param.15) | copy-start | bytes 3145732
  57.3 35.8 %all-to-all-start.1 = ((bf16[16,3,2,96,128]{4,3,2,1,0:T(8,128)(2,1)}), bf16[16,3,2,96,128]{4,3,2,1,0:T(8,128)(2,1)}, u32[]{:S(2)}, u32[]{:S(2)}) async-start(bf16[16,3,2,96,128]{4,3,2,1,0:T(8,128)(2,1)} %get-tuple-element.29), calls=%async_computation.1 | async-start | bytes 4718592 | tf_op jit(solution)/shard_map/all_to_all | solution.py:338
  70.6 4.3 %collective-permute-start = (bf16[4,768,256]{2,1,0:T(8,128)(2,1)}, bf16[4,768,256]{2,1,0:T(8,128)(2,1)S(1)}, u32[]{:S(2)}, u32[]{:S(2)}) collective-permute-start(bf16[4,768,256]{2,1,0:T(8,128)(2,1)} %fusion), channel_id=1, source_target_pairs={{0,16},{16,0},{32,48},{48,32},{64,80},{80,64},{96,112},{112,96},{1... | collective-permute-start | bytes 4718600 | tf_op jit(solution)/shard_map/ppermute | solution.py:330
  71.6 1.4 %copy-start.1 = (bf16[4,1,256,2,128]{2,4,3,0,1:T(8,128)(2,1)S(1)}, bf16[4,1,256,2,128]{2,4,3,0,1:T(8,128)(2,1)}, u32[]{:S(2)}) copy-start(bf16[4,1,256,2,128]{2,4,3,0,1:T(8,128)(2,1)} %copy.13) | copy-start | bytes 1572868
  96.4 2.7 %collective-permute-start.2 = (bf16[512,768]{1,0:T(8,128)(2,1)S(1)}, bf16[512,768]{1,0:T(8,128)(2,1)S(1)}, u32[]{:S(2)}, u32[]{:S(2)}) collective-permute-start(bf16[512,768]{1,0:T(8,128)(2,1)S(1)} %get-tuple-element.31.b_ref.refs_4_.refs_2_), channel_id=1, source_target_pairs={{0,16},{16,0},{32,48},{48,32},{64,80},{80,64},{96,112},{112,96},{1... | collective-permute-start | bytes 2359304 | tf_op jit(solution)/shard_map/ppermute | solution.py:341
  98.6 5.7 %collective-permute-start.1 = (bf16[512,768]{1,0:T(8,128)(2,1)S(1)}, bf16[512,768]{1,0:T(8,128)(2,1)S(1)}, u32[]{:S(2)}, u32[]{:S(2)}) collective-permute-start(bf16[512,768]{1,0:T(8,128)(2,1)S(1)} %unpack_last.1.a_ref.refs_2_), channel_id=1, source_target_pairs={{0,16},{16,0},{32,48},{48,32},{64,80},{80,64},{96,112},{112,96},{1... | collective-permute-start | bytes 2359304 | tf_op jit(solution)/shard_map/ppermute | solution.py:343
  100.1 10.8 %collective-permute-start.7 = (bf16[512,256]{1,0:T(8,128)(2,1)S(1)}, bf16[512,256]{1,0:T(8,128)(2,1)S(1)}, u32[]{:S(2)}, u32[]{:S(2)}) collective-permute-start(bf16[512,256]{1,0:T(8,128)(2,1)S(1)} %get-tuple-element.44), channel_id=1, source_target_pairs={{0,96},{16,112},{32,0},{48,16},{64,32},{80,48},{96,64},{112,80},{1... | collective-permute-start | bytes 786440 | tf_op jit(solution)/shard_map/ppermute | solution.py:349
  105.2 10.5 %collective-permute-start.3 = (bf16[512,256]{1,0:T(8,128)(2,1)S(1)}, bf16[512,256]{1,0:T(8,128)(2,1)S(1)}, u32[]{:S(2)}, u32[]{:S(2)}) collective-permute-start(bf16[512,256]{1,0:T(8,128)(2,1)S(1)} %get-tuple-element.40), channel_id=1, source_target_pairs={{0,32},{16,48},{32,64},{48,80},{64,96},{80,112},{96,0},{112,16},{1... | collective-permute-start | bytes 786440 | tf_op jit(solution)/shard_map/ppermute | solution.py:346
  105.3 13.4 %collective-permute-start.5 = (bf16[512,256]{1,0:T(8,128)(2,1)S(1)}, bf16[512,256]{1,0:T(8,128)(2,1)S(1)}, u32[]{:S(2)}, u32[]{:S(2)}) collective-permute-start(bf16[512,256]{1,0:T(8,128)(2,1)S(1)} %get-tuple-element.41), channel_id=1, source_target_pairs={{0,96},{16,112},{32,0},{48,16},{64,32},{80,48},{96,64},{112,80},{1... | collective-permute-start | bytes 786440 | tf_op jit(solution)/shard_map/ppermute | solution.py:347
  108.5 12.8 %collective-permute-start.6 = (bf16[512,256]{1,0:T(8,128)(2,1)S(1)}, bf16[512,256]{1,0:T(8,128)(2,1)S(1)}, u32[]{:S(2)}, u32[]{:S(2)}) collective-permute-start(bf16[512,256]{1,0:T(8,128)(2,1)S(1)} %get-tuple-element.42), channel_id=1, source_target_pairs={{0,32},{16,48},{32,64},{48,80},{64,96},{80,112},{96,0},{112,16},{1... | collective-permute-start | bytes 786440 | tf_op jit(solution)/shard_map/ppermute | solution.py:350
  111.0 10.3 %collective-permute-start.8 = (bf16[512,256]{1,0:T(8,128)(2,1)S(1)}, bf16[512,256]{1,0:T(8,128)(2,1)S(1)}, u32[]{:S(2)}, u32[]{:S(2)}) collective-permute-start(bf16[512,256]{1,0:T(8,128)(2,1)S(1)} %add_convert_fusion), channel_id=1, source_target_pairs={{0,96},{16,112},{32,0},{48,16},{64,32},{80,48},{96,64},{112,80},{1... | collective-permute-start | bytes 786440 | tf_op jit(solution)/shard_map/ppermute | solution.py:355
  115.8 9.9 %collective-permute-start.4 = (bf16[512,256]{1,0:T(8,128)(2,1)S(1)}, bf16[512,256]{1,0:T(8,128)(2,1)S(1)}, u32[]{:S(2)}, u32[]{:S(2)}) collective-permute-start(bf16[512,256]{1,0:T(8,128)(2,1)S(1)} %add_convert_fusion.1), channel_id=1, source_target_pairs={{0,32},{16,48},{32,64},{48,80},{64,96},{80,112},{96,0},{112,16},{1... | collective-permute-start | bytes 786440 | tf_op jit(solution)/shard_map/ppermute | solution.py:354

commit v4 on v3

--- a/solution.py
+++ b/solution.py
@@ -209,7 +209,7 @@
             copy.start()
             copies.append(copy)
     for h in range(2):
-        place_ref[h] = places(1, h, flat_ref)
+        place_ref[h] = places(0, h, flat_ref)
     for h in range(2):
         for copy in copies[3 * h : 3 * h + 3]:
             copy.wait()
@@ -233,7 +233,7 @@
 
 def unpack_last_kernel(flat_ref, rows_ref, own_ref):
     for h in range(2):
-        gather(h, rows_ref, own_ref, places(0, h, flat_ref))
+        gather(h, rows_ref, own_ref, places(1, h, flat_ref))
 
 
 def unpack_last(flat, rows):
@@ -274,18 +274,21 @@
     )(near(own_a), near(own_b))
 
 
-def project_kernel(plan, *refs):
+def project_kernel(plan, count, skip, *refs):
     mine_ref, theirs_ref = refs[:2]
-    grads, outs = refs[2 : len(refs) - len(plan)], refs[len(refs) - len(plan) :]
-    for (at, j), out in zip(plan, outs):
+    outs = refs[-len(plan) :]
+    grads, extra = refs[2 : 2 + count], refs[2 + count : -len(plan) - skip]
+    for i, ((at, j), out) in enumerate(zip(plan, outs)):
         total = dot(grads[at][...], mine_ref[j]) + dot(grads[at + 1][...], theirs_ref[j])
+        if extra and i == len(plan) - 1:
+            total = total + extra[0][...].astype(f32)
         out[...] = total.astype(out.dtype)
 
 
-def project(plan, types, mine, theirs, *grads):
-    return pl.pallas_call(
-        functools.partial(project_kernel, plan),
-        in_specs=[WHOLE] * (2 + len(grads)),
+def project(plan, types, mine, theirs, grads, extra=(), after=()):
+    return pl.pallas_call(
+        functools.partial(project_kernel, plan, len(grads), len(after)),
+        in_specs=[WHOLE] * (2 + len(grads) + len(extra)) + [pl.BlockSpec(memory_space=pl.ANY)] * len(after),
         out_specs=(WHOLE,) * len(plan),
         out_shape=tuple(pltpu.VMEM((HALF, QUARTER), kind) for kind in types),
         compiler_params=pltpu.CompilerParams(vmem_limit_bytes=6 * MIB),
@@ -293,19 +296,19 @@
             flops=len(plan) * 4 * HALF * QUARTER * 6 * WIDTH, bytes_accessed=10**6, transcendentals=0
         ),
         name="project",
-    )(*[near(x) for x in (mine, theirs, *grads)])
-
-
-def finish_kernel(a_ref, b_ref, a_up, a_down, b_up, b_down, out_ref):
-    for s, (own, up, down) in enumerate(((a_ref, a_up, a_down), (b_ref, b_up, b_down))):
-        total = own[...] + up[...].astype(f32) + down[...].astype(f32)
+    )(*[near(x) for x in (mine, theirs, *grads, *extra)], *after)
+
+
+def finish_kernel(a_ref, b_ref, a_up, b_down, out_ref):
+    for s, (own, got) in enumerate(((a_ref, a_up), (b_ref, b_down))):
+        total = own[...] + got[...].astype(f32)
         out_ref[:, HALF * s : HALF * (s + 1)] = total.T.astype(bf16)
 
 
 def finish(*parts):
     return pl.pallas_call(
         finish_kernel,
-        in_specs=[WHOLE] * 6,
+        in_specs=[WHOLE] * 4,
         out_specs=WHOLE,
         out_shape=jax.ShapeDtypeStruct((QUARTER, TOK), bf16),
         compiler_params=pltpu.CompilerParams(vmem_limit_bytes=6 * MIB),
@@ -337,26 +340,25 @@
     key_sums = jnp.transpose(sums, (1, 0, 2))
     home = lax.all_to_all(back, "seq", split_axis=0, concat_axis=0, tiled=True)
     flat, mine, theirs = lax.optimization_barrier((flat, mine, theirs))
-    own_b, rows = unpack_first(flat, home)
+    own_a, rows = unpack_first(flat, home)
+    other_a = lax.ppermute(own_a, "head", swap)
+    own_b = unpack_last(flat, rows)
     other_b = lax.ppermute(own_b, "head", swap)
-    own_a = unpack_last(flat, rows)
-    other_a = lax.ppermute(own_a, "head", swap)
-
-    far_a, down_a = project(((0, 2), (0, 3)), (bf16, bf16), mine, theirs, own_a, other_a)
-    far_a = lax.ppermute(far_a, "head", up)
-    down_a = lax.ppermute(down_a, "head", down)
-    far_b, up_b = project(((0, 2), (0, 1)), (bf16, bf16), mine, theirs, own_b, other_b)
+
+    half_a, half_b = (own_a, other_a), (own_b, other_b)
+    first, second = project(((0, 2), (0, 3)), (bf16, bf16), mine, theirs, half_a)
+    far_a = lax.ppermute(first, "head", up)
+    down_a = lax.ppermute(second, "head", down)
+    far_b, up_b = project(((0, 2), (0, 1)), (bf16, bf16), mine, theirs, half_b, after=(first,))
     far_b = lax.ppermute(far_b, "head", down)
     up_b = lax.ppermute(up_b, "head", up)
-    next_a, last_b = project(
-        ((0, 1), (2, 3)), (f32,) * 2, mine, theirs, own_a, other_a, own_b, other_b
-    )
+    (last_b,) = project(((0, 3),), (f32,), mine, theirs, half_b)
+    (sum_b,) = project(((0, 0),), (f32,), mine, theirs, half_b, (up_b,))
+    down_b = lax.ppermute((last_b + far_b.astype(f32)).astype(bf16), "head", down)
+    (next_a,) = project(((0, 1),), (f32,), mine, theirs, half_a)
+    (sum_a,) = project(((0, 0),), (f32,), mine, theirs, half_a, (down_a,))
     up_a = lax.ppermute((next_a + far_a.astype(f32)).astype(bf16), "head", up)
-    down_b = lax.ppermute((last_b + far_b.astype(f32)).astype(bf16), "head", down)
-    own_sum_a, own_sum_b = project(
-        ((0, 0), (2, 0)), (f32,) * 2, mine, theirs, own_a, other_a, own_b, other_b
-    )
-    input_grad = finish(own_sum_a, own_sum_b, up_a, down_a, up_b, down_b)
+    input_grad = finish(sum_a, sum_b, up_a, down_b)
     grads = [x.reshape(TOK, 2, WIDTH) for x in merge(own_a, own_b)]
     return (*grads, input_grad, key_sums)
 

time: 127 us -> 126 us (level)
  waiting for transfers between devices: 27.7 us -> 26.1 us
    ppermute x1, waiting for transfers between devices: 4.36 us -> 0.01 us  [shards(): up_a = lax.ppermute((next_a + far_a.astype(f32)).astype(bf16), 'head', up)]
    ppermute x1, waiting for transfers between devices: 1.41 us -> 4.38 us  [shards(): far_b = lax.ppermute(far_b, 'head', down)]
    ppermute x1, waiting for transfers between devices: 2.66 us -> 0.01 us  [shards(): up_b = lax.ppermute(up_b, 'head', up)]
    ppermute x1, waiting for transfers between devices: 0.01 us -> 1.88 us  [shards(): lax.ppermute((last_b + far_b.astype(f32)).astype(bf16), 'head', down)]
    pallas_call x5 -> x7, Pallas kernels: 4.97 us -> 5.26 us  [the longest x6 4.25 us: project(): pl.pallas_call(functools.partial(project_kernel, plan, len(grads), len(af...]
  transfers between devices with their start and end apart: 10 -> 10, of which waited for: 5 -> 4; matrix products, arithmetic and copies ran while one was open for 10% -> 10% of each run, Pallas kernels for 6% -> 6%
where the time goes in v4:
time: 126 us; the launch traced here: 125 us
  blocking collectives  46.4 us (37%)
  waiting for transfers between devices  26.1 us (21%)
  Pallas kernels  22 us (17%)
  starting transfers between devices  16.4 us (13%)
  local copies, waits for them, and re-layouts  8.77 us (7%)
  other arithmetic  4.9 us (4%)
    all_to_all x1, blocking collectives, shards(): got = lax.all_to_all(sent, 'seq', split_axis=0, concat_axis=0, tiled=True)  46.4 us
    all_to_all x1, waiting for transfers between devices, shards(): home = lax.all_to_all(back, 'seq', split_axis=0, concat_axis=0, tiled=True)  18.2 us
    dynamic_slice x8, local copies, waits for them, and re-layouts, blocks(): lax.dynamic_index_in_dim(w, which, 1, keepdims=False)  8.07 us
    pallas_call x1, Pallas kernels, pack(): pl.pallas_call(pack_kernel, in_specs=[WHOLE] + [pl.BlockSpec(memory_space...  5.53 us
    all_to_all x1, starting transfers between devices, shards(): home = lax.all_to_all(back, 'seq', split_axis=0, concat_axis=0, tiled=True)  4.59 us
    ppermute x1, waiting for transfers between devices, shards(): far_b = lax.ppermute(far_b, 'head', down)  4.38 us
    pallas_call x6, Pallas kernels, project(): pl.pallas_call(functools.partial(project_kernel, plan, len(grads), len(af...  4.25 us
    pallas_call x1, Pallas kernels, attend(): pl.pallas_call(attend_kernel, in_specs=[WHOLE], out_specs=(pl.BlockSpec(m...  4.11 us
  transfers between devices with their start and end apart: 10, of which 4 were waited for; matrix products, arithmetic and copies ran while one was open for 10% of the time, Pallas kernels for 6%

profile of v4, /device:TPU:0, one launch (start us, length us, event | category | flops | bytes accessed | tf_op | source)
XLA Modules:
  0.0 125.5 jit_solution(12495431700234352711)
XLA Ops:
  0.6 0.7 copy-done
  1.3 5.5 %pack.1 = (bf16[16,4,2,96,128]{4,3,2,1,0:T(8,128)(2,1)S(1)}, s32[2,1,1024]{2,1,0:T(1,128)S(1)}) custom-call(s32[2,1,1024]{2,1,0:T(1,128)S(1)} %bitcast.24, bf16[2048,128]{1,0:T(8,128)(2,1)} %bitcast.36, bf16[2048,128]{1,0:T(8,128)(2,1)} %bitcast.37, bf16[2048,128]{1,0:T(8,128)(2,1)} %bitcast.38, bf16[2048,128]{1,0:T(8,128)(2,1)} %bitcast.39), custom_call_target="tpu_custom_call" | custom-call | tf_op jit(solution)/shard_map/pack/pallas_call | solution.py:107
  6.9 46.4 %all_to_all.10.in_ref = bf16[16,4,2,96,128]{4,3,2,1,0:T(8,128)(2,1)S(1)} all-to-all(bf16[16,4,2,96,128]{4,3,2,1,0:T(8,128)(2,1)S(1)} %get-tuple-element.24), channel_id=1, replica_groups=mesh['head'=8,'seq'=16] {'seq'}, dimensions={0} | all-to-all | bytes 6291456 | tf_op jit(solution)/shard_map/all_to_all | solution.py:338
  53.3 4.1 %attend.1 = (bf16[16,3,2,96,128]{4,3,2,1,0:T(8,128)(2,1)}, f32[12,2,128]{2,1,0:T(2,128)}) custom-call(bf16[16,4,2,96,128]{4,3,2,1,0:T(8,128)(2,1)S(1)} %all_to_all.10.in_ref), custom_call_target="tpu_custom_call" | custom-call | tf_op jit(solution)/shard_map/attend/pallas_call | solution.py:172
  57.4 4.6 %all-to-all-start.1 = ((bf16[16,3,2,96,128]{4,3,2,1,0:T(8,128)(2,1)}), bf16[16,3,2,96,128]{4,3,2,1,0:T(8,128)(2,1)}, u32[]{:S(2)}, u32[]{:S(2)}) async-start(bf16[16,3,2,96,128]{4,3,2,1,0:T(8,128)(2,1)} %get-tuple-element.25), calls=%async_computation.1 | async-start | bytes 4718592 | tf_op jit(solution)/shard_map/all_to_all | solution.py:341
  62.1 0.7 constant_dynamic-slice_fusion.2
  63.2 3.1 %constant_dynamic-slice_fusion = (bf16[4,1,256,2,128]{4,3,2,1,0:T(2,128)(2,1)S(1)}, bf16[4,1,256,2,128]{4,3,2,1,0:T(2,128)(2,1)S(1)}, bf16[4,1,256,2,128]{4,3,2,...) fusion(bf16[4,2,256,2,128]{4,3,2,1,0:T(2,128)(2,1)} %bitcast.33, s32[]{:T(128)S(6)} %select_n.34, s32[]{:T(128)S(6)} %select_n.32, ...), kind=kLoop, calls=%fused_computation.10 | loop fusion | bytes 4194312 | tf_op jit(solution)/shard_map/jit(dynamic_index_in_dim)/dynamic_slice | solution.py:328
  66.2 1.1 copy.18
  67.7 1.2 pad_maximum_fusion.1
  68.9 1.8 %fusion = bf16[4,768,256]{2,1,0:T(8,128)(2,1)} fusion(s32[]{:T(128)S(6)} %select_n.38, bf16[4,768,256]{2,1,0:T(8,128)(2,1)S(1)} %bitcast.26), kind=kLoop, calls=%fused_computation.4 | loop fusion | flops 786432 | bytes 3145732 | tf_op jit(solution)/shard_map/jit(_roll_dynamic)/concatenate | solution.py:330
  70.7 1.1 copy.13
  71.7 1.1 copy.15
  73.2 1.2 pad_maximum_fusion
  74.4 0.6 fusion.1.refs_0_
  75.0 18.2 %all-to-all-done.1.home_ref = bf16[16,3,2,96,128]{4,3,2,1,0:T(8,128)(2,1)} async-done(((bf16[16,3,2,96,128]{4,3,2,1,0:T(8,128)(2,1)}), bf16[16,3,2,96,128]{4,3,2,1,0:T(8,128)(2,1)}, u32[]{:S(2)}, u32[]{:S(2)}) %all-to-all-start.1) | async-done | bytes 2359328 | tf_op jit(solution)/shard_map/all_to_all | solution.py:341
  93.2 3.2 %unpack_first.1 = (bf16[512,768]{1,0:T(8,128)(2,1)S(1)}, bf16[2,3,16,96,128]{4,3,2,1,0:T(8,128)(2,1)S(1)}) custom-call(s32[2,1,1024]{2,1,0:T(1,128)S(1)} %get-tuple-element.23.flat_ref, bf16[16,3,2,96,128]{4,3,2,1,0:T(8,128)(2,1)} %all-to-all-done.1.home_ref), custom_call_target="tpu_custom_call" | custom-call | tf_op jit(solution)/shard_map/unpack_first/pallas_call | solution.py:220
  96.6 2.0 %unpack_last.1.b_ref.refs_2_ = bf16[512,768]{1,0:T(8,128)(2,1)S(1)} custom-call(s32[2,1,1024]{2,1,0:T(1,128)S(1)} %get-tuple-element.23.flat_ref, bf16[2,3,16,96,128]{4,3,2,1,0:T(8,128)(2,1)S(1)} %get-tuple-element.27.rows_ref), custom_call_target="tpu_custom_call" | custom-call | tf_op jit(solution)/shard_map/unpack_last/pallas_call | solution.py:240
  98.6 0.6 collective-permute-start.3
  99.2 1.0 project.6
  100.2 2.0 %collective-permute-start.5 = (bf16[512,256]{1,0:T(8,128)(2,1)S(1)}, bf16[512,256]{1,0:T(8,128)(2,1)S(1)}, u32[]{:S(2)}, u32[]{:S(2)}) collective-permute-start(bf16[512,256]{1,0:T(8,128)(2,1)S(1)} %get-tuple-element.34.refs_4_), channel_id=1, source_target_pairs={{0,32},{16,48},{32,64},{48,80},{64,96},{80,112},{96,0},{112,16},{1... | collective-permute-start | bytes 786440 | tf_op jit(solution)/shard_map/ppermute | solution.py:350
  102.2 2.2 %collective-permute-start.2 = (bf16[512,256]{1,0:T(8,128)(2,1)S(1)}, bf16[512,256]{1,0:T(8,128)(2,1)S(1)}, u32[]{:S(2)}, u32[]{:S(2)}) collective-permute-start(bf16[512,256]{1,0:T(8,128)(2,1)S(1)} %get-tuple-element.33), channel_id=1, source_target_pairs={{0,96},{16,112},{32,0},{48,16},{64,32},{80,48},{96,64},{112,80},{1... | collective-permute-start | bytes 786440 | tf_op jit(solution)/shard_map/ppermute | solution.py:351
  104.4 1.0 project.8
  105.5 3.2 %collective-permute-start.7 = (bf16[512,256]{1,0:T(8,128)(2,1)S(1)}, bf16[512,256]{1,0:T(8,128)(2,1)S(1)}, u32[]{:S(2)}, u32[]{:S(2)}) collective-permute-start(bf16[512,256]{1,0:T(8,128)(2,1)S(1)} %get-tuple-element.36), channel_id=1, source_target_pairs={{0,96},{16,112},{32,0},{48,16},{64,32},{80,48},{96,64},{112,80},{1... | collective-permute-start | bytes 786440 | tf_op jit(solution)/shard_map/ppermute | solution.py:353
  109.3 0.6 project.10
  109.8 1.6 %collective-permute-done.5 = bf16[512,256]{1,0:T(8,128)(2,1)S(1)} collective-permute-done((bf16[512,256]{1,0:T(8,128)(2,1)S(1)}, bf16[512,256]{1,0:T(8,128)(2,1)S(1)}, u32[]{:S(2)}, u32[]{:S(2)}) %collective-permute-start.5) | collective-permute-done | bytes 262176 | tf_op jit(solution)/shard_map/ppermute | solution.py:350
  111.6 4.4 %collective-permute-done.7 = bf16[512,256]{1,0:T(8,128)(2,1)S(1)} collective-permute-done((bf16[512,256]{1,0:T(8,128)(2,1)S(1)}, bf16[512,256]{1,0:T(8,128)(2,1)S(1)}, u32[]{:S(2)}, u32[]{:S(2)}) %collective-permute-start.7) | collective-permute-done | bytes 262176 | tf_op jit(solution)/shard_map/ppermute | solution.py:353
  116.0 3.6 %collective-permute-start.8 = (bf16[512,256]{1,0:T(8,128)(2,1)S(1)}, bf16[512,256]{1,0:T(8,128)(2,1)S(1)}, u32[]{:S(2)}, u32[]{:S(2)}) collective-permute-start(bf16[512,256]{1,0:T(8,128)(2,1)S(1)} %add_convert_fusion), channel_id=1, source_target_pairs={{0,96},{16,112},{32,0},{48,16},{64,32},{80,48},{96,64},{112,80},{1... | collective-permute-start | bytes 786440 | tf_op jit(solution)/shard_map/ppermute | solution.py:357
  119.6 1.8 %merge.1 = (bf16[2048,128]{1,0:T(8,128)(2,1)}, bf16[2048,128]{1,0:T(8,128)(2,1)}, bf16[2048,128]{1,0:T(8,128)(2,1)}) custom-call(bf16[512,768]{1,0:T(8,128)(2,1)S(1)} %get-tuple-element.26.a_ref.refs_2_, bf16[512,768]{1,0:T(8,128)(2,1)S(1)} %unpack_last.1.b_ref.refs_2_), custom_call_target="tpu_custom_call" | custom-call | flops 1000000000 | bytes 3000000 | tf_op jit(solution)/shard_map/merge/pallas_call | solution.py:266
  121.4 0.6 project.7.a_ref
  122.0 0.6 project.9.b_ref
  122.6 1.9 %collective-permute-done.8.b_down = bf16[512,256]{1,0:T(8,128)(2,1)S(1)} collective-permute-done((bf16[512,256]{1,0:T(8,128)(2,1)S(1)}, bf16[512,256]{1,0:T(8,128)(2,1)S(1)}, u32[]{:S(2)}, u32[]{:S(2)}) %collective-permute-start.8) | collective-permute-done | bytes 262176 | tf_op jit(solution)/shard_map/ppermute | solution.py:357
  124.5 1.0 finish.1
  (21 shorter events, 2.1 us)
Async XLA Ops:
  0.6 0.7 copy-start
  57.4 4.7 %copy-start.2 = (bf16[2048,2,128]{2,1,0:T(2,128)(2,1)S(1)}, bf16[2048,2,128]{2,1,0:T(2,128)(2,1)}, u32[]{:S(2)}) copy-start(bf16[2048,2,128]{2,1,0:T(2,128)(2,1)} %param.15) | copy-start | bytes 3145732
  57.4 35.8 %all-to-all-start.1 = ((bf16[16,3,2,96,128]{4,3,2,1,0:T(8,128)(2,1)}), bf16[16,3,2,96,128]{4,3,2,1,0:T(8,128)(2,1)}, u32[]{:S(2)}, u32[]{:S(2)}) async-start(bf16[16,3,2,96,128]{4,3,2,1,0:T(8,128)(2,1)} %get-tuple-element.25), calls=%async_computation.1 | async-start | bytes 4718592 | tf_op jit(solution)/shard_map/all_to_all | solution.py:341
  70.7 4.3 %collective-permute-start = (bf16[4,768,256]{2,1,0:T(8,128)(2,1)}, bf16[4,768,256]{2,1,0:T(8,128)(2,1)S(1)}, u32[]{:S(2)}, u32[]{:S(2)}) collective-permute-start(bf16[4,768,256]{2,1,0:T(8,128)(2,1)} %fusion), channel_id=1, source_target_pairs={{0,16},{16,0},{32,48},{48,32},{64,80},{80,64},{96,112},{112,96},{1... | collective-permute-start | bytes 4718600 | tf_op jit(solution)/shard_map/ppermute | solution.py:333
  71.7 1.4 %copy-start.1 = (bf16[4,1,256,2,128]{2,4,3,0,1:T(8,128)(2,1)S(1)}, bf16[4,1,256,2,128]{2,4,3,0,1:T(8,128)(2,1)}, u32[]{:S(2)}) copy-start(bf16[4,1,256,2,128]{2,4,3,0,1:T(8,128)(2,1)} %copy.13) | copy-start | bytes 1572868
  96.5 2.7 %collective-permute-start.1 = (bf16[512,768]{1,0:T(8,128)(2,1)S(1)}, bf16[512,768]{1,0:T(8,128)(2,1)S(1)}, u32[]{:S(2)}, u32[]{:S(2)}) collective-permute-start(bf16[512,768]{1,0:T(8,128)(2,1)S(1)} %get-tuple-element.26.a_ref.refs_2_), channel_id=1, source_target_pairs={{0,16},{16,0},{32,48},{48,32},{64,80},{80,64},{96,112},{112,96},{1... | collective-permute-start | bytes 2359304 | tf_op jit(solution)/shard_map/ppermute | solution.py:344
  98.6 5.8 %collective-permute-start.3 = (bf16[512,768]{1,0:T(8,128)(2,1)S(1)}, bf16[512,768]{1,0:T(8,128)(2,1)S(1)}, u32[]{:S(2)}, u32[]{:S(2)}) collective-permute-start(bf16[512,768]{1,0:T(8,128)(2,1)S(1)} %unpack_last.1.b_ref.refs_2_), channel_id=1, source_target_pairs={{0,16},{16,0},{32,48},{48,32},{64,80},{80,64},{96,112},{112,96},{1... | collective-permute-start | bytes 2359304 | tf_op jit(solution)/shard_map/ppermute | solution.py:346
  100.2 11.2 %collective-permute-start.5 = (bf16[512,256]{1,0:T(8,128)(2,1)S(1)}, bf16[512,256]{1,0:T(8,128)(2,1)S(1)}, u32[]{:S(2)}, u32[]{:S(2)}) collective-permute-start(bf16[512,256]{1,0:T(8,128)(2,1)S(1)} %get-tuple-element.34.refs_4_), channel_id=1, source_target_pairs={{0,32},{16,48},{32,64},{48,80},{64,96},{80,112},{96,0},{112,16},{1... | collective-permute-start | bytes 786440 | tf_op jit(solution)/shard_map/ppermute | solution.py:350
  102.2 19.2 %collective-permute-start.2 = (bf16[512,256]{1,0:T(8,128)(2,1)S(1)}, bf16[512,256]{1,0:T(8,128)(2,1)S(1)}, u32[]{:S(2)}, u32[]{:S(2)}) collective-permute-start(bf16[512,256]{1,0:T(8,128)(2,1)S(1)} %get-tuple-element.33), channel_id=1, source_target_pairs={{0,96},{16,112},{32,0},{48,16},{64,32},{80,48},{96,64},{112,80},{1... | collective-permute-start | bytes 786440 | tf_op jit(solution)/shard_map/ppermute | solution.py:351
  105.4 16.6 %collective-permute-start.4 = (bf16[512,256]{1,0:T(8,128)(2,1)S(1)}, bf16[512,256]{1,0:T(8,128)(2,1)S(1)}, u32[]{:S(2)}, u32[]{:S(2)}) collective-permute-start(bf16[512,256]{1,0:T(8,128)(2,1)S(1)} %get-tuple-element.35), channel_id=1, source_target_pairs={{0,32},{16,48},{32,64},{48,80},{64,96},{80,112},{96,0},{112,16},{1... | collective-permute-start | bytes 786440 | tf_op jit(solution)/shard_map/ppermute | solution.py:354
  105.5 10.5 %collective-permute-start.7 = (bf16[512,256]{1,0:T(8,128)(2,1)S(1)}, bf16[512,256]{1,0:T(8,128)(2,1)S(1)}, u32[]{:S(2)}, u32[]{:S(2)}) collective-permute-start(bf16[512,256]{1,0:T(8,128)(2,1)S(1)} %get-tuple-element.36), channel_id=1, source_target_pairs={{0,96},{16,112},{32,0},{48,16},{64,32},{80,48},{96,64},{112,80},{1... | collective-permute-start | bytes 786440 | tf_op jit(solution)/shard_map/ppermute | solution.py:353
  111.5 11.1 %collective-permute-start.6 = (bf16[512,256]{1,0:T(8,128)(2,1)S(1)}, bf16[512,256]{1,0:T(8,128)(2,1)S(1)}, u32[]{:S(2)}, u32[]{:S(2)}) collective-permute-start(bf16[512,256]{1,0:T(8,128)(2,1)S(1)} %add_convert_fusion.1), channel_id=1, source_target_pairs={{0,32},{16,48},{32,64},{48,80},{64,96},{80,112},{96,0},{112,16},{1... | collective-permute-start | bytes 786440 | tf_op jit(solution)/shard_map/ppermute | solution.py:360
  116.0 8.5 %collective-permute-start.8 = (bf16[512,256]{1,0:T(8,128)(2,1)S(1)}, bf16[512,256]{1,0:T(8,128)(2,1)S(1)}, u32[]{:S(2)}, u32[]{:S(2)}) collective-permute-start(bf16[512,256]{1,0:T(8,128)(2,1)S(1)} %add_convert_fusion), channel_id=1, source_target_pairs={{0,96},{16,112},{32,0},{48,16},{64,32},{80,48},{96,64},{112,80},{1... | collective-permute-start | bytes 786440 | tf_op jit(solution)/shard_map/ppermute | solution.py:357

commit v5 on v4

--- a/solution.py
+++ b/solution.py
@@ -75,15 +75,19 @@
         flat = ids[h] * SLOTS + jnp.concatenate(ranks[h], axis=1).astype(jnp.int32)
         flat_ref[h] = flat
         flats.append(flat)
-    for copy in copies:
-        copy.wait()
     i, j = iota((256, 256), 0), iota((256, 256), 1)
     split = (j == jnp.where(i < 128, 2 * i, 2 * i - 255)).astype(f32).astype(bf16)
-    for b in range(TOK // 128):
-        block = jnp.concatenate([pairs_ref[x, 256 * b : 256 * (b + 1), :] for x in range(4)], axis=1)
-        parted = dot(split, block).astype(bf16)
-        rows_ref[0, 128 * b : 128 * (b + 1), :] = parted[:128]
-        rows_ref[1, 128 * b : 128 * (b + 1), :] = parted[128:]
+    for x in (0, 2):
+        copies[x].wait()
+        copies[x + 1].wait()
+        for b in range(TOK // 128):
+            block = jnp.concatenate(
+                [pairs_ref[y, 256 * b : 256 * (b + 1), :] for y in (x, x + 1)], axis=1
+            )
+            parted = dot(split, block).astype(bf16)
+            at = slice(WIDTH * x, WIDTH * (x + 2))
+            rows_ref[0, 128 * b : 128 * (b + 1), at] = parted[:128]
+            rows_ref[1, 128 * b : 128 * (b + 1), at] = parted[128:]
     step = PACK_DSTS * RUN
     slot = iota((step, TOK), 0)
     groups = (PACK_DSTS * CL_DEV, SLOTS, WIDTH)
@@ -299,21 +303,26 @@
     )(*[near(x) for x in (mine, theirs, *grads, *extra)], *after)
 
 
-def finish_kernel(a_ref, b_ref, a_up, b_down, out_ref):
-    for s, (own, got) in enumerate(((a_ref, a_up), (b_ref, b_down))):
-        total = own[...] + got[...].astype(f32)
-        out_ref[:, HALF * s : HALF * (s + 1)] = total.T.astype(bf16)
-
-
-def finish(*parts):
-    return pl.pallas_call(
-        finish_kernel,
-        in_specs=[WHOLE] * 4,
-        out_specs=WHOLE,
+def finish_kernel(half, own_ref, got_ref, *refs):
+    out_ref, turned_ref, sem = refs[-3:]
+    turned_ref[...] = (own_ref[...] + got_ref[...].astype(f32)).T.astype(bf16)
+    copy = pltpu.make_async_copy(turned_ref, out_ref.at[:, pl.ds(HALF * half, HALF)], sem)
+    copy.start()
+    copy.wait()
+
+
+def finish(half, own, got, *whole):
+    far = pl.BlockSpec(memory_space=pltpu.HBM)
+    return pl.pallas_call(
+        functools.partial(finish_kernel, half),
+        in_specs=[WHOLE] * 2 + [far] * len(whole),
+        out_specs=far,
         out_shape=jax.ShapeDtypeStruct((QUARTER, TOK), bf16),
+        scratch_shapes=[pltpu.VMEM((QUARTER, HALF), bf16), pltpu.SemaphoreType.DMA],
+        input_output_aliases={2: 0} if whole else {},
         compiler_params=pltpu.CompilerParams(vmem_limit_bytes=6 * MIB),
         name="finish",
-    )(*[near(x) for x in parts])
+    )(near(own), near(got), *whole)
 
 
 def shards(queries, keys, values, out_grad, cluster_ids, query_weight, key_weight, value_weight):
@@ -358,7 +367,7 @@
     (next_a,) = project(((0, 1),), (f32,), mine, theirs, half_a)
     (sum_a,) = project(((0, 0),), (f32,), mine, theirs, half_a, (down_a,))
     up_a = lax.ppermute((next_a + far_a.astype(f32)).astype(bf16), "head", up)
-    input_grad = finish(sum_a, sum_b, up_a, down_b)
+    input_grad = finish(1, sum_b, down_b, finish(0, sum_a, up_a))
     grads = [x.reshape(TOK, 2, WIDTH) for x in merge(own_a, own_b)]
     return (*grads, input_grad, key_sums)
 

time: 126 us -> 126 us (level)
  transfers between devices with their start and end apart: 10 -> 10, of which waited for: 4 -> 4; matrix products, arithmetic and copies ran while one was open for 10% -> 10% of each run, Pallas kernels for 6% -> 7%
where the time goes in v5:
time: 126 us; the launch traced here: 125 us
  blocking collectives  46.4 us (37%)
  waiting for transfers between devices  25.2 us (20%)
  Pallas kernels  22.5 us (18%)
  starting transfers between devices  16.4 us (13%)
  local copies, waits for them, and re-layouts  8.77 us (7%)
  other arithmetic  4.89 us (4%)
    all_to_all x1, blocking collectives, shards(): got = lax.all_to_all(sent, 'seq', split_axis=0, concat_axis=0, tiled=True)  46.4 us
    all_to_all x1, waiting for transfers between devices, shards(): home = lax.all_to_all(back, 'seq', split_axis=0, concat_axis=0, tiled=True)  18.2 us
    dynamic_slice x8, local copies, waits for them, and re-layouts, blocks(): lax.dynamic_index_in_dim(w, which, 1, keepdims=False)  8.07 us
    pallas_call x1, Pallas kernels, pack(): pl.pallas_call(pack_kernel, in_specs=[WHOLE] + [pl.BlockSpec(memory_space...  5.38 us
    all_to_all x1, starting transfers between devices, shards(): home = lax.all_to_all(back, 'seq', split_axis=0, concat_axis=0, tiled=True)  4.59 us
    ppermute x1, waiting for transfers between devices, shards(): far_b = lax.ppermute(far_b, 'head', down)  4.4 us
    pallas_call x6, Pallas kernels, project(): pl.pallas_call(functools.partial(project_kernel, plan, len(grads), len(af...  4.25 us
    pallas_call x1, Pallas kernels, attend(): pl.pallas_call(attend_kernel, in_specs=[WHOLE], out_specs=(pl.BlockSpec(m...  4.04 us
  transfers between devices with their start and end apart: 10, of which 4 were waited for; matrix products, arithmetic and copies ran while one was open for 10% of the time, Pallas kernels for 7%

profile of v5, /device:TPU:0, one launch (start us, length us, event | category | flops | bytes accessed | tf_op | source)
XLA Modules:
  0.0 125.3 jit_solution(12597277105182178177)
XLA Ops:
  0.6 0.7 copy-done
  1.3 5.4 %pack.1 = (bf16[16,4,2,96,128]{4,3,2,1,0:T(8,128)(2,1)S(1)}, s32[2,1,1024]{2,1,0:T(1,128)S(1)}) custom-call(s32[2,1,1024]{2,1,0:T(1,128)S(1)} %bitcast.24, bf16[2048,128]{1,0:T(8,128)(2,1)} %bitcast.36, bf16[2048,128]{1,0:T(8,128)(2,1)} %bitcast.37, bf16[2048,128]{1,0:T(8,128)(2,1)} %bitcast.38, bf16[2048,128]{1,0:T(8,128)(2,1)} %bitcast.39), custom_call_target="tpu_custom_call" | custom-call | tf_op jit(solution)/shard_map/pack/pallas_call | solution.py:111
  6.7 46.4 %all_to_all.10.in_ref = bf16[16,4,2,96,128]{4,3,2,1,0:T(8,128)(2,1)S(1)} all-to-all(bf16[16,4,2,96,128]{4,3,2,1,0:T(8,128)(2,1)S(1)} %get-tuple-element.24), channel_id=1, replica_groups=mesh['head'=8,'seq'=16] {'seq'}, dimensions={0} | all-to-all | bytes 6291456 | tf_op jit(solution)/shard_map/all_to_all | solution.py:347
  53.1 4.0 %attend.1 = (bf16[16,3,2,96,128]{4,3,2,1,0:T(8,128)(2,1)}, f32[12,2,128]{2,1,0:T(2,128)}) custom-call(bf16[16,4,2,96,128]{4,3,2,1,0:T(8,128)(2,1)S(1)} %all_to_all.10.in_ref), custom_call_target="tpu_custom_call" | custom-call | tf_op jit(solution)/shard_map/attend/pallas_call | solution.py:176
  57.2 4.6 %all-to-all-start.1 = ((bf16[16,3,2,96,128]{4,3,2,1,0:T(8,128)(2,1)}), bf16[16,3,2,96,128]{4,3,2,1,0:T(8,128)(2,1)}, u32[]{:S(2)}, u32[]{:S(2)}) async-start(bf16[16,3,2,96,128]{4,3,2,1,0:T(8,128)(2,1)} %get-tuple-element.25), calls=%async_computation.1 | async-start | bytes 4718592 | tf_op jit(solution)/shard_map/all_to_all | solution.py:350
  61.8 0.7 constant_dynamic-slice_fusion.2
  63.0 3.1 %constant_dynamic-slice_fusion = (bf16[4,1,256,2,128]{4,3,2,1,0:T(2,128)(2,1)S(1)}, bf16[4,1,256,2,128]{4,3,2,1,0:T(2,128)(2,1)S(1)}, bf16[4,1,256,2,128]{4,3,2,...) fusion(bf16[4,2,256,2,128]{4,3,2,1,0:T(2,128)(2,1)} %bitcast.33, s32[]{:T(128)S(6)} %select_n.34, s32[]{:T(128)S(6)} %select_n.32, ...), kind=kLoop, calls=%fused_computation.10 | loop fusion | bytes 4194312 | tf_op jit(solution)/shard_map/jit(dynamic_index_in_dim)/dynamic_slice | solution.py:337
  66.0 1.1 copy.19
  67.5 1.2 pad_maximum_fusion.1
  68.7 1.8 %fusion = bf16[4,768,256]{2,1,0:T(8,128)(2,1)} fusion(s32[]{:T(128)S(6)} %select_n.38, bf16[4,768,256]{2,1,0:T(8,128)(2,1)S(1)} %bitcast.26), kind=kLoop, calls=%fused_computation.4 | loop fusion | flops 786432 | bytes 3145732 | tf_op jit(solution)/shard_map/jit(_roll_dynamic)/concatenate | solution.py:339
  70.5 1.1 copy.14
  71.5 1.1 copy.16
  73.0 1.2 pad_maximum_fusion
  74.2 0.6 fusion.1.refs_0_
  74.8 18.2 %all-to-all-done.1.home_ref = bf16[16,3,2,96,128]{4,3,2,1,0:T(8,128)(2,1)} async-done(((bf16[16,3,2,96,128]{4,3,2,1,0:T(8,128)(2,1)}), bf16[16,3,2,96,128]{4,3,2,1,0:T(8,128)(2,1)}, u32[]{:S(2)}, u32[]{:S(2)}) %all-to-all-start.1) | async-done | bytes 2359328 | tf_op jit(solution)/shard_map/all_to_all | solution.py:350
  93.0 3.2 %unpack_first.1 = (bf16[512,768]{1,0:T(8,128)(2,1)S(1)}, bf16[2,3,16,96,128]{4,3,2,1,0:T(8,128)(2,1)S(1)}) custom-call(s32[2,1,1024]{2,1,0:T(1,128)S(1)} %get-tuple-element.23.flat_ref, bf16[16,3,2,96,128]{4,3,2,1,0:T(8,128)(2,1)} %all-to-all-done.1.home_ref), custom_call_target="tpu_custom_call" | custom-call | tf_op jit(solution)/shard_map/unpack_first/pallas_call | solution.py:224
  96.4 2.0 %unpack_last.1.b_ref.refs_2_ = bf16[512,768]{1,0:T(8,128)(2,1)S(1)} custom-call(s32[2,1,1024]{2,1,0:T(1,128)S(1)} %get-tuple-element.23.flat_ref, bf16[2,3,16,96,128]{4,3,2,1,0:T(8,128)(2,1)S(1)} %get-tuple-element.27.rows_ref), custom_call_target="tpu_custom_call" | custom-call | tf_op jit(solution)/shard_map/unpack_last/pallas_call | solution.py:244
  99.0 1.0 project.6
  100.0 2.0 %collective-permute-start.7 = (bf16[512,256]{1,0:T(8,128)(2,1)S(1)}, bf16[512,256]{1,0:T(8,128)(2,1)S(1)}, u32[]{:S(2)}, u32[]{:S(2)}) collective-permute-start(bf16[512,256]{1,0:T(8,128)(2,1)S(1)} %get-tuple-element.33.refs_4_), channel_id=1, source_target_pairs={{0,32},{16,48},{32,64},{48,80},{64,96},{80,112},{96,0},{112,16},{1... | collective-permute-start | bytes 786440 | tf_op jit(solution)/shard_map/ppermute | solution.py:359
  102.0 2.2 %collective-permute-start.6 = (bf16[512,256]{1,0:T(8,128)(2,1)S(1)}, bf16[512,256]{1,0:T(8,128)(2,1)S(1)}, u32[]{:S(2)}, u32[]{:S(2)}) collective-permute-start(bf16[512,256]{1,0:T(8,128)(2,1)S(1)} %get-tuple-element.36), channel_id=1, source_target_pairs={{0,96},{16,112},{32,0},{48,16},{64,32},{80,48},{96,64},{112,80},{1... | collective-permute-start | bytes 786440 | tf_op jit(solution)/shard_map/ppermute | solution.py:360
  104.1 1.0 project.7
  105.2 3.2 %collective-permute-start.4 = (bf16[512,256]{1,0:T(8,128)(2,1)S(1)}, bf16[512,256]{1,0:T(8,128)(2,1)S(1)}, u32[]{:S(2)}, u32[]{:S(2)}) collective-permute-start(bf16[512,256]{1,0:T(8,128)(2,1)S(1)} %get-tuple-element.35), channel_id=1, source_target_pairs={{0,96},{16,112},{32,0},{48,16},{64,32},{80,48},{96,64},{112,80},{1... | collective-permute-start | bytes 786440 | tf_op jit(solution)/shard_map/ppermute | solution.py:362
  109.0 0.6 project.11
  109.6 1.6 %collective-permute-done.7 = bf16[512,256]{1,0:T(8,128)(2,1)S(1)} collective-permute-done((bf16[512,256]{1,0:T(8,128)(2,1)S(1)}, bf16[512,256]{1,0:T(8,128)(2,1)S(1)}, u32[]{:S(2)}, u32[]{:S(2)}) %collective-permute-start.7) | collective-permute-done | bytes 262176 | tf_op jit(solution)/shard_map/ppermute | solution.py:359
  111.3 4.4 %collective-permute-done.4 = bf16[512,256]{1,0:T(8,128)(2,1)S(1)} collective-permute-done((bf16[512,256]{1,0:T(8,128)(2,1)S(1)}, bf16[512,256]{1,0:T(8,128)(2,1)S(1)}, u32[]{:S(2)}, u32[]{:S(2)}) %collective-permute-start.4) | collective-permute-done | bytes 262176 | tf_op jit(solution)/shard_map/ppermute | solution.py:362
  115.8 3.6 %collective-permute-start.5 = (bf16[512,256]{1,0:T(8,128)(2,1)S(1)}, bf16[512,256]{1,0:T(8,128)(2,1)S(1)}, u32[]{:S(2)}, u32[]{:S(2)}) collective-permute-start(bf16[512,256]{1,0:T(8,128)(2,1)S(1)} %add_convert_fusion.1), channel_id=1, source_target_pairs={{0,96},{16,112},{32,0},{48,16},{64,32},{80,48},{96,64},{112,80},{1... | collective-permute-start | bytes 786440 | tf_op jit(solution)/shard_map/ppermute | solution.py:366
  119.3 1.8 %merge.1 = (bf16[2048,128]{1,0:T(8,128)(2,1)}, bf16[2048,128]{1,0:T(8,128)(2,1)}, bf16[2048,128]{1,0:T(8,128)(2,1)}) custom-call(bf16[512,768]{1,0:T(8,128)(2,1)S(1)} %get-tuple-element.26.a_ref.refs_2_, bf16[512,768]{1,0:T(8,128)(2,1)S(1)} %unpack_last.1.b_ref.refs_2_), custom_call_target="tpu_custom_call" | custom-call | flops 1000000000 | bytes 3000000 | tf_op jit(solution)/shard_map/merge/pallas_call | solution.py:270
  121.2 0.6 project.10.own_ref
  121.8 0.6 project.8.own_ref
  122.4 0.9 finish.2.refs_0_
  123.2 1.0 collective-permute-done.5.got_ref
  124.2 0.8 finish.3
  (22 shorter events, 2.6 us)
Async XLA Ops:
  0.6 0.7 copy-start
  57.2 4.7 %copy-start.2 = (bf16[2048,2,128]{2,1,0:T(2,128)(2,1)S(1)}, bf16[2048,2,128]{2,1,0:T(2,128)(2,1)}, u32[]{:S(2)}) copy-start(bf16[2048,2,128]{2,1,0:T(2,128)(2,1)} %param.15) | copy-start | bytes 3145732
  57.2 35.8 %all-to-all-start.1 = ((bf16[16,3,2,96,128]{4,3,2,1,0:T(8,128)(2,1)}), bf16[16,3,2,96,128]{4,3,2,1,0:T(8,128)(2,1)}, u32[]{:S(2)}, u32[]{:S(2)}) async-start(bf16[16,3,2,96,128]{4,3,2,1,0:T(8,128)(2,1)} %get-tuple-element.25), calls=%async_computation.1 | async-start | bytes 4718592 | tf_op jit(solution)/shard_map/all_to_all | solution.py:350
  70.5 4.3 %collective-permute-start = (bf16[4,768,256]{2,1,0:T(8,128)(2,1)}, bf16[4,768,256]{2,1,0:T(8,128)(2,1)S(1)}, u32[]{:S(2)}, u32[]{:S(2)}) collective-permute-start(bf16[4,768,256]{2,1,0:T(8,128)(2,1)} %fusion), channel_id=1, source_target_pairs={{0,16},{16,0},{32,48},{48,32},{64,80},{80,64},{96,112},{112,96},{1... | collective-permute-start | bytes 4718600 | tf_op jit(solution)/shard_map/ppermute | solution.py:342
  71.5 1.4 %copy-start.1 = (bf16[4,1,256,2,128]{2,4,3,0,1:T(8,128)(2,1)S(1)}, bf16[4,1,256,2,128]{2,4,3,0,1:T(8,128)(2,1)}, u32[]{:S(2)}) copy-start(bf16[4,1,256,2,128]{2,4,3,0,1:T(8,128)(2,1)} %copy.14) | copy-start | bytes 1572868
  96.3 2.7 %collective-permute-start.2 = (bf16[512,768]{1,0:T(8,128)(2,1)S(1)}, bf16[512,768]{1,0:T(8,128)(2,1)S(1)}, u32[]{:S(2)}, u32[]{:S(2)}) collective-permute-start(bf16[512,768]{1,0:T(8,128)(2,1)S(1)} %get-tuple-element.26.a_ref.refs_2_), channel_id=1, source_target_pairs={{0,16},{16,0},{32,48},{48,32},{64,80},{80,64},{96,112},{112,96},{1... | collective-permute-start | bytes 2359304 | tf_op jit(solution)/shard_map/ppermute | solution.py:353
  98.4 5.7 %collective-permute-start.1 = (bf16[512,768]{1,0:T(8,128)(2,1)S(1)}, bf16[512,768]{1,0:T(8,128)(2,1)S(1)}, u32[]{:S(2)}, u32[]{:S(2)}) collective-permute-start(bf16[512,768]{1,0:T(8,128)(2,1)S(1)} %unpack_last.1.b_ref.refs_2_), channel_id=1, source_target_pairs={{0,16},{16,0},{32,48},{48,32},{64,80},{80,64},{96,112},{112,96},{1... | collective-permute-start | bytes 2359304 | tf_op jit(solution)/shard_map/ppermute | solution.py:355
  100.0 11.2 %collective-permute-start.7 = (bf16[512,256]{1,0:T(8,128)(2,1)S(1)}, bf16[512,256]{1,0:T(8,128)(2,1)S(1)}, u32[]{:S(2)}, u32[]{:S(2)}) collective-permute-start(bf16[512,256]{1,0:T(8,128)(2,1)S(1)} %get-tuple-element.33.refs_4_), channel_id=1, source_target_pairs={{0,32},{16,48},{32,64},{48,80},{64,96},{80,112},{96,0},{112,16},{1... | collective-permute-start | bytes 786440 | tf_op jit(solution)/shard_map/ppermute | solution.py:359
  102.0 19.2 %collective-permute-start.6 = (bf16[512,256]{1,0:T(8,128)(2,1)S(1)}, bf16[512,256]{1,0:T(8,128)(2,1)S(1)}, u32[]{:S(2)}, u32[]{:S(2)}) collective-permute-start(bf16[512,256]{1,0:T(8,128)(2,1)S(1)} %get-tuple-element.36), channel_id=1, source_target_pairs={{0,96},{16,112},{32,0},{48,16},{64,32},{80,48},{96,64},{112,80},{1... | collective-permute-start | bytes 786440 | tf_op jit(solution)/shard_map/ppermute | solution.py:360
  105.1 16.6 %collective-permute-start.3 = (bf16[512,256]{1,0:T(8,128)(2,1)S(1)}, bf16[512,256]{1,0:T(8,128)(2,1)S(1)}, u32[]{:S(2)}, u32[]{:S(2)}) collective-permute-start(bf16[512,256]{1,0:T(8,128)(2,1)S(1)} %get-tuple-element.34), channel_id=1, source_target_pairs={{0,32},{16,48},{32,64},{48,80},{64,96},{80,112},{96,0},{112,16},{1... | collective-permute-start | bytes 786440 | tf_op jit(solution)/shard_map/ppermute | solution.py:363
  105.2 10.5 %collective-permute-start.4 = (bf16[512,256]{1,0:T(8,128)(2,1)S(1)}, bf16[512,256]{1,0:T(8,128)(2,1)S(1)}, u32[]{:S(2)}, u32[]{:S(2)}) collective-permute-start(bf16[512,256]{1,0:T(8,128)(2,1)S(1)} %get-tuple-element.35), channel_id=1, source_target_pairs={{0,96},{16,112},{32,0},{48,16},{64,32},{80,48},{96,64},{112,80},{1... | collective-permute-start | bytes 786440 | tf_op jit(solution)/shard_map/ppermute | solution.py:362
  111.2 11.1 %collective-permute-start.8 = (bf16[512,256]{1,0:T(8,128)(2,1)S(1)}, bf16[512,256]{1,0:T(8,128)(2,1)S(1)}, u32[]{:S(2)}, u32[]{:S(2)}) collective-permute-start(bf16[512,256]{1,0:T(8,128)(2,1)S(1)} %add_convert_fusion), channel_id=1, source_target_pairs={{0,32},{16,48},{32,64},{48,80},{64,96},{80,112},{96,0},{112,16},{1... | collective-permute-start | bytes 786440 | tf_op jit(solution)/shard_map/ppermute | solution.py:369
  115.8 8.5 %collective-permute-start.5 = (bf16[512,256]{1,0:T(8,128)(2,1)S(1)}, bf16[512,256]{1,0:T(8,128)(2,1)S(1)}, u32[]{:S(2)}, u32[]{:S(2)}) collective-permute-start(bf16[512,256]{1,0:T(8,128)(2,1)S(1)} %add_convert_fusion.1), channel_id=1, source_target_pairs={{0,96},{16,112},{32,0},{48,16},{64,32},{80,48},{96,64},{112,80},{1... | collective-permute-start | bytes 786440 | tf_op jit(solution)/shard_map/ppermute | solution.py:366
